TPU v7x, 128 devices: a whole 4x4x4 slice. The times are simulated.
128 devices in a mesh: seq: 16 (over z, y_lo, core), tp: 8 (over x, y_hi).
Axes of the slice: x: 4, y: 4 (y_hi: 2, y_lo: 2; y = y_hi * 2 + y_lo), z: 4, core: 2. Of those that a mesh axis runs over, the one named last changes fastest.
Arguments:
- queries: bfloat16 [8192, 4096], P('seq', 'tp'), may hold values from -6 to 6
- audio_keys: bfloat16 [2048, 4096], P('seq', 'tp'), may hold values from -6 to 6
- audio_values: bfloat16 [2048, 4096], P('seq', 'tp'), may hold values from -12 to 12
- out_weight: bfloat16 [4096, 8192], P('tp'), may hold values from -0.09375 to 0.09375
- mix_gate: float32 [1], replicated, may hold values from 0.3 to 1.2
- block_mask: int32 [64, 16], P('seq'), may hold values from 0 to 1, as said below
- cotangent: bfloat16 [8192, 8192], P(('seq', 'tp')), may hold values from -24 to 24
Outputs:
- layer_out: bfloat16 [8192, 8192], P(('seq', 'tp'))
- grad_queries: bfloat16 [8192, 4096], P('seq', 'tp')
- grad_keys: bfloat16 [2048, 4096], P('seq', 'tp')
- grad_values: bfloat16 [2048, 4096], P('seq', 'tp')
- grad_weight: bfloat16 [4096, 8192], P('tp', 'seq')
Inputs may be any that keep to these rules, and one draw needn't show every extreme that they name: Every row of block_mask holds at least one 1.
All inputs are finite; a program needn't handle non-finite values.
Results may differ from a plain program's by a relative error of at most 0.025.
Values may be sent and summed in bfloat16 or wider, within the bound.
A program may use at most 128 MiB of HBM per device.

v0:
```python
from functools import partial

import jax
import jax.numpy as jnp
from jax import lax
from jax.sharding import PartitionSpec as P

HD = 128
BLK = 128


negative_fill = -1e30


def fold_step(state_now, pieces, offset, query_heads, allowed, score_scale):
    key_rows, value_rows = pieces
    width_rows = key_rows.shape[0]
    key_heads = key_rows.reshape(width_rows, -1, HD)
    value_heads = value_rows.reshape(width_rows, -1, HD)
    scores = (
        jnp.einsum("thd,ahd->hta", query_heads, key_heads, preferred_element_type=jnp.float32)
        * score_scale
    )
    window = allowed[None, :, :]
    row_best, row_total, weighted = state_now
    block_best = jnp.max(jnp.where(window, scores, negative_fill), axis=2)
    new_best = jnp.maximum(row_best, block_best)
    weights = jnp.where(window, jnp.exp(scores - new_best[:, :, None]), 0.0)
    row_total = jnp.sum(weights, axis=2)
    weighted = jnp.einsum(
        "hta,ahd->htd",
        weights.astype(jnp.bfloat16),
        value_heads,
        preferred_element_type=jnp.float32,
    )
    return (new_best, row_total, weighted)


def per_device(queries, audio_keys, audio_values, out_weight, mix_gate, block_mask, cotangent):
    score_scale = HD ** (-0.5)
    tokens = queries.shape[0]
    feature_count = queries.shape[1]
    head_count = feature_count // HD
    query_heads = queries.reshape(tokens, head_count, HD)
    mask_rows = jnp.repeat(block_mask, BLK, axis=0)
    allowed = jnp.repeat(mask_rows, BLK, axis=1) > 0
    start_state = (
        jnp.full((head_count, tokens), negative_fill, jnp.float32),
        jnp.zeros((head_count, tokens), jnp.float32),
        jnp.zeros((head_count, tokens, HD), jnp.float32),
    )
    fold_once = partial(
        fold_step, query_heads=query_heads, allowed=allowed, score_scale=score_scale
    )
    row_best, row_total, weighted = fold_once(
        start_state,
        (
            lax.all_gather(audio_keys, "seq", axis=0, tiled=True),
            lax.all_gather(audio_values, "seq", axis=0, tiled=True),
        ),
        jnp.int32(0),
    )
    heads_out = (
        jnp.transpose(weighted / row_total[:, :, None], (1, 0, 2))
        .reshape(tokens, feature_count)
        .astype(jnp.bfloat16)
    )
    log_total = row_best + jnp.log(row_total)
    gate_value = jnp.tanh(mix_gate[0])
    layer_sum = lax.psum_scatter(
        jnp.dot(heads_out, out_weight, preferred_element_type=jnp.float32).astype(jnp.bfloat16),
        "tp",
        scatter_dimension=0,
        tiled=True,
    ).astype(jnp.float32)
    layer_out = (gate_value * layer_sum).astype(jnp.bfloat16)
    full_grad = lax.all_gather(cotangent, "tp", axis=0, tiled=True)
    grad_heads = (
        gate_value
        * jnp.einsum("td,kd->tk", full_grad, out_weight, preferred_element_type=jnp.float32)
    ).astype(jnp.bfloat16)
    weight_term = gate_value * jnp.einsum(
        "tk,td->kd", heads_out, full_grad, preferred_element_type=jnp.float32
    )
    grad_weight = lax.psum_scatter(
        weight_term.astype(jnp.bfloat16), "seq", scatter_dimension=1, tiled=True
    )
    key_all, value_all = (
        lax.all_gather(audio_keys, "seq", axis=0, tiled=True),
        lax.all_gather(audio_values, "seq", axis=0, tiled=True),
    )
    key_heads = key_all.reshape(-1, head_count, HD)
    value_heads = value_all.reshape(-1, head_count, HD)
    scores = (
        jnp.einsum("thd,ahd->hta", query_heads, key_heads, preferred_element_type=jnp.float32)
        * score_scale
    )
    probs = jnp.where(allowed[None, :, :], jnp.exp(scores - log_total[:, :, None]), 0.0)
    grad_heads3 = grad_heads.reshape(tokens, head_count, HD)
    grad_probs = jnp.einsum(
        "thd,ahd->hta", grad_heads3, value_heads, preferred_element_type=jnp.float32
    )
    delta_rows = jnp.einsum(
        "thd,thd->ht",
        grad_heads3,
        heads_out.reshape(tokens, head_count, HD),
        preferred_element_type=jnp.float32,
    )
    grad_scores = (probs * (grad_probs - delta_rows[:, :, None])).astype(jnp.bfloat16)
    prob_rounded = probs.astype(jnp.bfloat16)
    grad_queries = (
        (
            score_scale
            * jnp.einsum("hta,ahd->thd", grad_scores, key_heads, preferred_element_type=jnp.float32)
        )
        .reshape(tokens, feature_count)
        .astype(jnp.bfloat16)
    )
    span_rows = audio_keys.shape[0] * lax.axis_size("seq")
    key_term = score_scale * jnp.einsum(
        "hta,thd->ahd", grad_scores, query_heads, preferred_element_type=jnp.float32
    )
    value_term = jnp.einsum(
        "hta,thd->ahd", prob_rounded, grad_heads3, preferred_element_type=jnp.float32
    )
    both_grads = lax.psum_scatter(
        jnp.concatenate(
            [
                key_term.reshape(span_rows, feature_count),
                value_term.reshape(span_rows, feature_count),
            ],
            axis=1,
        ).astype(jnp.bfloat16),
        "seq",
        scatter_dimension=0,
        tiled=True,
    ).astype(jnp.float32)
    grad_keys = both_grads[:, :feature_count].astype(jnp.bfloat16)
    grad_values = both_grads[:, feature_count:].astype(jnp.bfloat16)
    return (layer_out, grad_queries, grad_keys, grad_values, grad_weight)


def solution(mesh):
    in_specs = (
        P("seq", "tp"),
        P("seq", "tp"),
        P("seq", "tp"),
        P("tp", None),
        P(),
        P("seq", None),
        P(("seq", "tp"), None),
    )
    out_specs = (
        P(("seq", "tp"), None),
        P("seq", "tp"),
        P("seq", "tp"),
        P("seq", "tp"),
        P("tp", "seq"),
    )
    return jax.shard_map(
        per_device, mesh=mesh, in_specs=in_specs, out_specs=out_specs, check_vma=False
    )
```

profile of v0, /device:TPU:1, one launch (start us, length us, event | category | flops | bytes accessed | tf_op | source)
XLA Modules:
  0.0 541.8 jit_solution(13899247454757285208)
XLA Ops:
  7.2 0.7 all-gather.6.cloned.1.call-update
  7.9 1.7 copy.21
  9.7 0.7 all-gather.8.cloned.1.call-update
  11.1 1.3 copy.41
  12.4 0.7 broadcast_compare_fusion
  13.1 3.5 broadcast_in_dim.38
  16.6 0.6 copy.44
  17.2 30.5 %all-gather.6.cloned.1.call-done = bf16[2048,512]{1,0:T(8,128)(2,1)} async-done(((bf16[128,512]{1,0:T(8,128)(2,1)}), bf16[2048,512]{1,0:T(8,128)(2,1)}) %all-gather.6.cloned.1.call-update) | async-done | bytes 2097168 | tf_op jit(solution)/shard_map/all_gather | solution.py:59
  47.7 4.0 copy.24
  51.7 35.3 %all-gather.4.cloned.1.call-done = bf16[2048,512]{0,1:T(8,128)(2,1)} async-done(((bf16[128,512]{0,1:T(8,128)(2,1)}), bf16[2048,512]{0,1:T(8,128)(2,1)}) %all-gather.4.cloned.1.call-update) | async-done | bytes 2097168 | tf_op jit(solution)/shard_map/all_gather | solution.py:58
  87.0 5.1 select_reduce_fusion
  92.1 4.6 fusion
  96.7 1.1 copy-done
  98.8 98.8 %all-gather.8.cloned.1.call-done = bf16[512,8192]{1,0:T(8,128)(2,1)} async-done(((bf16[64,8192]{1,0:T(8,128)(2,1)}), bf16[512,8192]{1,0:T(8,128)(2,1)}) %all-gather.8.cloned.1.call-update) | async-done | bytes 8388624 | tf_op jit(solution)/shard_map/all_gather | solution.py:77
  197.6 10.4 %fusion.16 = bf16[512,512]{0,1:T(8,128)(2,1)S(1)} fusion(bf16[512,8192]{1,0:T(8,128)(2,1)} %all-gather.8.cloned.1.call-done, bf16[512,8192]{1,0:T(8,128)(2,1)} %param.10, f32[]{:T(128)} %bitcast.2), kind=kOutput, calls=%fused_computation.22 | convolution fusion | flops 4295491584 | bytes 17301508 | tf_op jit(solution)/shard_map/td,kd->tk/dot_general | solution.py:80
  208.7 6.6 %fusion.17 = (f32[4,512]{1,0:T(4,128)}, bf16[512,4,128]{0,2,1:T(8,128)(2,1)}) fusion(bf16[512,512]{0,1:T(8,128)(2,1)S(1)} %fusion.16, f32[512,4]{0,1:T(4,128)S(1)} %bitcast.64, bf16[2048,4,128]{0,2,1:T(8,128)(2,1)S(1)} %bitcast.58, f32[4,512,2048]{2,1,0:T(8,128)S(1)} %copy-done.1, f32[4,512]{1,0:T(4,128)S(1)} %copy-done.8, pred[512,2048]{1,0:T(8,128)(4,1)S(1)} %bitcast.48), kind=kOutput, calls=%fused_computation.24 | convolution fusion | flops 1092089856 | bytes 20996096 | tf_op jit(solution)/shard_map/hta,ahd->htd/dot_general | solution.py:30
  215.3 7.1 %fusion.9 = bf16[4,128,2048]{2,1,0:T(8,128)(2,1)} fusion(bf16[512,4,128]{0,2,1:T(8,128)(2,1)} %bitcast.65, f32[4,512,2048]{2,1,0:T(8,128)S(1)} %copy-done.1, f32[4,512]{1,0:T(4,128)} %log_add_fusion, pred[512,2048]{1,0:T(8,128)(4,1)S(1)} %bitcast.49), kind=kOutput, calls=%fused_computation.16 | convolution fusion | flops 1091567616 | bytes 20455424 | tf_op jit(solution)/shard_map/hta,thd->ahd/dot_general | solution.py:123
  222.5 12.4 %multiply_convert_fusion.1 = bf16[4,512,2048]{2,1,0:T(8,128)(2,1)} fusion(f32[4,512,2048]{2,1,0:T(8,128)} %copy-done, f32[4,512]{1,0:T(4,128)} %get-tuple-element.19, f32[4,512]{1,0:T(4,128)S(1)} %copy-done.9, pred[512,2048]{1,0:T(8,128)(4,1)S(1)} %bitcast.50, bf16[512,4,128]{0,2,1:T(8,128)(2,1)} %bitcast.66, bf16[2048,4,128]{0,2,1:T(8,128)(2,1)} %bitcast.57), kind=kOutput, calls=%fused_computation.1 | convolution fusion | flops 1098907648 | bytes 28852224 | tf_op jit(solution)/shard_map/thd,ahd->hta/dot_general | solution.py:100
  234.9 6.1 %multiply_convert_fusion.2 = bf16[4,2048,128]{1,2,0:T(8,128)(2,1)} fusion(bf16[512,4,128]{0,2,1:T(8,128)(2,1)S(1)} %bitcast.53, bf16[4,512,2048]{2,1,0:T(8,128)(2,1)} %multiply_convert_fusion.1), kind=kOutput, calls=%fused_computation.14 | convolution fusion | flops 1075838976 | bytes 11010048 | tf_op jit(solution)/shard_map/hta,thd->ahd/dot_general | solution.py:120
  241.0 2.9 copy.28
  243.9 4.0 copy.29
  247.8 4.2 pad_maximum_fusion
  252.1 10.1 %convolution_convert_fusion = bf16[512,8192]{1,0:T(8,128)(2,1)} fusion(bf16[512,512]{0,1:T(8,128)(2,1)S(1)} %bitcast.60, bf16[512,8192]{1,0:T(8,128)(2,1)} %param.10), kind=kOutput, calls=%fused_computation.8 | convolution fusion | flops 4299161600 | bytes 17301504 | tf_op jit(solution)/shard_map/dot_general | solution.py:71
  262.3 10.4 %multiply_convert_fusion = bf16[512,8192]{1,0:T(8,128)(2,1)} fusion(bf16[512,512]{0,1:T(8,128)(2,1)S(1)} %bitcast.61, bf16[512,8192]{1,0:T(8,128)(2,1)} %all-gather.8.cloned.1.call-done, f32[]{:T(128)} %bitcast.2), kind=kOutput, calls=%fused_computation | convolution fusion | flops 4303355904 | bytes 17301508 | tf_op jit(solution)/shard_map/tk,td->kd/dot_general | solution.py:82
  272.7 1.6 copy-done.4
  274.3 6.4 %fusion.15 = bf16[4,512,128]{1,2,0:T(8,128)(2,1)S(1)} fusion(bf16[4,512,2048]{2,1,0:T(8,128)(2,1)} %multiply_convert_fusion.1, bf16[2048,4,128]{0,2,1:T(8,128)(2,1)S(1)} %bitcast.55), kind=kOutput, calls=%fused_computation.21 | convolution fusion | flops 1074266112 | bytes 11010048 | tf_op jit(solution)/shard_map/hta,ahd->thd/dot_general | solution.py:114
  280.7 1.0 copy.30
  281.7 36.5 %reduce-scatter.6.cloned.1.call-done = bf16[128,1024]{1,0:T(8,128)(2,1)} async-done(((bf16[2048,1024]{1,0:T(8,128)(2,1)}), bf16[128,1024]{1,0:T(8,128)(2,1)}) %reduce-scatter.6.cloned.1.call-update) | async-done | bytes 262160 | tf_op jit(solution)/shard_map/reduce_scatter | solution.py:126
  318.2 1.7 fusion.24
  319.9 117.6 %reduce-scatter.4.cloned.1.call-done = bf16[64,8192]{1,0:T(8,128)(2,1)} async-done(((bf16[512,8192]{1,0:T(8,128)(2,1)}), bf16[64,8192]{1,0:T(8,128)(2,1)}) %reduce-scatter.4.cloned.1.call-update) | async-done | bytes 1048592 | tf_op jit(solution)/shard_map/reduce_scatter | solution.py:70
  437.5 2.4 multiply_convert_fusion.3
  439.9 95.1 %reduce-scatter.8.cloned.1.call-done = bf16[512,512]{1,0:T(8,128)(2,1)} async-done(((bf16[512,8192]{1,0:T(8,128)(2,1)}), bf16[512,512]{1,0:T(8,128)(2,1)}) %reduce-scatter.8.cloned.1.call-update) | async-done | bytes 524304 | tf_op jit(solution)/shard_map/reduce_scatter | solution.py:85
  (33 shorter events, 2.0 us)
Async XLA Ops:
  7.2 40.6 %all-gather.6.cloned.1.call-start = ((), (), s32[]{:S(2)}) async-start(), calls=%async_computation.4 | async-start | bytes 2228224 | tf_op jit(solution)/shard_map/all_gather | solution.py:59
  7.9 79.1 %all-gather.4.cloned.1.call-start = ((), (), s32[]{:S(2)}) async-start(), calls=%async_computation.3 | async-start | bytes 2228224 | tf_op jit(solution)/shard_map/all_gather | solution.py:58
  9.6 188.0 %all-gather.8.cloned.1.call-start = ((), (), s32[]{:S(2)}) async-start(), calls=%async_computation.6 | async-start | bytes 9437184 | tf_op jit(solution)/shard_map/all_gather | solution.py:77
  10.4 307.9 %reduce-scatter.6.cloned.1.call-start = ((), (), s32[]{:S(2)}) async-start(), calls=%async_computation.7 | async-start | bytes 4456448 | tf_op jit(solution)/shard_map/reduce_scatter | solution.py:126
  12.4 79.7 %copy-start.2 = (bf16[512,512]{0,1:T(8,128)(2,1)}, bf16[512,512]{0,1:T(8,128)(2,1)S(1)}, u32[]{:S(2)}) copy-start(bf16[512,512]{0,1:T(8,128)(2,1)S(1)} %copy.41) | copy-start | bytes 1572868
  92.1 5.7 %copy-start = (f32[4,512,2048]{2,1,0:T(8,128)}, f32[4,512,2048]{2,1,0:T(8,128)S(1)}, u32[]{:S(2)}) copy-start(f32[4,512,2048]{2,1,0:T(8,128)S(1)} %get-tuple-element.18) | copy-start | bytes 50331652
  92.1 6.1 %copy-start.7 = (f32[4,512]{1,0:T(4,128)}, f32[4,512]{1,0:T(4,128)S(1)}, u32[]{:S(2)}) copy-start(f32[4,512]{1,0:T(4,128)S(1)} %broadcast_maximum_fusion) | copy-start | bytes 24580
  197.6 10.5 %copy-start.1 = (f32[4,512,2048]{2,1,0:T(8,128)S(1)}, f32[4,512,2048]{2,1,0:T(8,128)}, u32[]{:S(2)}) copy-start(f32[4,512,2048]{2,1,0:T(8,128)} %copy-done) | copy-start | bytes 50331652
  197.6 11.1 %copy-start.5 = (bf16[2048,512]{0,1:T(8,128)(2,1)S(1)}, bf16[2048,512]{0,1:T(8,128)(2,1)}, u32[]{:S(2)}) copy-start(bf16[2048,512]{0,1:T(8,128)(2,1)} %copy.24) | copy-start | bytes 6291460
  197.6 11.1 %copy-start.8 = (f32[4,512]{1,0:T(4,128)S(1)}, f32[4,512]{1,0:T(4,128)}, u32[]{:S(2)}) copy-start(f32[4,512]{1,0:T(4,128)} %copy-done.7) | copy-start | bytes 24580
  208.0 7.3 %copy-start.10 = (bf16[512,512]{0,1:T(8,128)(2,1)}, bf16[512,512]{0,1:T(8,128)(2,1)S(1)}, u32[]{:S(2)}) copy-start(bf16[512,512]{0,1:T(8,128)(2,1)S(1)} %fusion.16) | copy-start | bytes 1572868
  215.3 7.1 %copy-start.9 = (f32[4,512]{1,0:T(4,128)S(1)}, f32[4,512]{1,0:T(4,128)}, u32[]{:S(2)}) copy-start(f32[4,512]{1,0:T(4,128)} %log_add_fusion) | copy-start | bytes 24580
  222.5 12.4 %copy-start.3 = (bf16[512,512]{0,1:T(8,128)(2,1)S(1)}, bf16[512,512]{0,1:T(8,128)(2,1)}, u32[]{:S(2)}) copy-start(bf16[512,512]{0,1:T(8,128)(2,1)} %copy-done.2) | copy-start | bytes 1572868
  243.8 8.3 %copy-start.6 = (bf16[512,4,128]{0,2,1:T(8,128)(2,1)S(1)}, bf16[512,4,128]{0,2,1:T(8,128)(2,1)}, u32[]{:S(2)}) copy-start(bf16[512,4,128]{0,2,1:T(8,128)(2,1)} %get-tuple-element.20) | copy-start | bytes 1572868
  252.1 185.4 %reduce-scatter.4.cloned.1.call-start = ((), (), s32[]{:S(2)}) async-start(), calls=%async_computation.5 | async-start | bytes 9437184 | tf_op jit(solution)/shard_map/reduce_scatter | solution.py:70
  262.3 272.7 %reduce-scatter.8.cloned.1.call-start = ((), (), s32[]{:S(2)}) async-start(), calls=%async_computation.8 | async-start | bytes 8912896 | tf_op jit(solution)/shard_map/reduce_scatter | solution.py:85
  272.7 1.6 copy-start.4
Sparse Core Ops, SparseCore 0:
  9.7 37.9 all-gather.5
  49.9 37.0 all-gather.3
  89.3 108.2 all-gather.7
  252.2 65.9 reduce-scatter.5
  321.9 115.5 reduce-scatter.3
  440.4 94.5 reduce-scatter.7
where the time goes:
time: 544 us; the launch traced here: 542 us
  waiting for transfers between devices  415 us (76%)
  matrix products  74.6 us (14%)
  local copies, waits for them, and re-layouts  24.3 us (4%)
  between operations  14.9 us (3%)
  other arithmetic  12.5 us (2%)
    reduce_scatter x1, waiting for transfers between devices, per_device(): lax.psum_scatter(jnp.dot(heads_out, out_weight, preferred_element_type=jn...  118 us
    all_gather x1, waiting for transfers between devices, per_device(): full_grad = lax.all_gather(cotangent, 'tp', axis=0, tiled=True)  98.8 us
    reduce_scatter x1, waiting for transfers between devices, per_device(): lax.psum_scatter(weight_term.astype(jnp.bfloat16), 'seq', scatter_dimensi...  95.1 us
    reduce_scatter x1, waiting for transfers between devices, per_device(): lax.psum_scatter(jnp.concatenate([key_term.reshape(span_rows, feature_cou...  36.5 us
    all_gather x1, waiting for transfers between devices, per_device(): lax.all_gather(audio_keys, 'seq', axis=0, tiled=True)  35.3 us
    all_gather x1, waiting for transfers between devices, per_device(): lax.all_gather(audio_values, 'seq', axis=0, tiled=True)  30.5 us
    dot_general x1, matrix products, per_device(): jnp.einsum('thd,ahd->hta', grad_heads3, value_heads, preferred_element_ty...  12.4 us
  transfers between devices with their start and end apart: 6, of which 6 were waited for; matrix products, arithmetic and copies ran while one was open for 10% of the time, Pallas kernels for 0%

commit v1 on v0

v1 whole, which is shorter than its diff:
```python
import jax
import jax.numpy as jnp
from jax import lax
from jax.experimental import pallas as pl
from jax.experimental.pallas import tpu as pltpu
from jax.sharding import PartitionSpec as P

HD = 128
BLK = 128
CH = 8
WC = 1024
HALF = 512
TOK = 512
AUD = 2048
SCALE = HD ** (-0.5)
C2 = SCALE * 1.4426950408889634
NEG = -1e30
BF = jnp.bfloat16
F32 = jnp.float32
MESH = pl.DeviceIdType.MESH

NT = (((1,), (1,)), ((), ()))
NN = (((1,), (0,)), ((), ()))
TN = (((0,), (0,)), ((), ()))

AGY, AGP, AGM, AFP, AFM, SIB, GW, F1, F2, R1, R2, YX = range(12)


def dot(a, b, dims):
    return lax.dot_general(a, b, dims, preferred_element_type=F32)


def kernel(
    q_hbm, k_hbm, v_hbm, w_hbm, gate_ref, mask_ref, cot_hbm,
    layer_ref, dq_ref, dk_ref, dv_ref, gw_ref,
    w, cot, cot_sib, kb, vb, q2, mask2, ht, hrow, gh_acc, gh_own, gh2,
    sc, pb, lse, delta, dq_acc, dq_out, dq_in, f1b, f2b, r1b, r2b, ys, yr, gw_out, gw_in, kv_out, kv_in,
    ss, rs, ks, kr, vs, vr, ds_, dr, es, er, ls,
):
    s = lax.axis_index("seq")
    t = lax.axis_index("tp")
    core = s % 2
    chip = s // 2
    x = t // 2
    yh = t % 2
    xn, xb, xf = (x + 1) % 4, (x + 3) % 4, (x + 2) % 4
    sib = (s + 1 - 2 * core, t)
    nxt = (s, xn * 2 + yh)
    prv = (s, xb * 2 + yh)
    par = (s, x * 2 + 1 - yh)

    def rows(start, size):
        return pl.ds(pl.multiple_of(start, size), size)

    def cols(start, size):
        return pl.ds(pl.multiple_of(start, 128), size)

    def chunk(i):
        return (chip + i) % CH

    def copy(kind, i, src, dst, dev):
        return pltpu.make_async_remote_copy(
            src_ref=src, dst_ref=dst, send_sem=ss.at[kind, i], recv_sem=rs.at[kind, i],
            device_id=dev, device_id_type=MESH,
        )

    def got(kind, i, dst):
        copy(kind, i, dst, dst, nxt).wait_recv()

    def sent(kind, i, src):
        copy(kind, i, src, src, nxt).wait_send()

    barrier = pltpu.get_barrier_semaphore()
    for dev in (nxt, prv, par):
        pl.semaphore_signal(barrier, inc=1, device_id=dev, device_id_type=MESH)

    def greet(j, c):
        pl.semaphore_signal(barrier, inc=1, device_id=((s + j) % 16, t), device_id_type=MESH)
        return c

    lax.fori_loop(1, 16, greet, 0)

    def own_piece(i):
        return pltpu.make_async_copy(
            cot_hbm.at[:, cols(chunk(i) * WC, WC)], cot.at[i, rows(t * 64, 64), :], ls.at[i]
        )

    def start_piece(i, c):
        own_piece(i).start()
        return c

    lax.fori_loop(0, CH, start_piece, 0)
    w_copy = pltpu.make_async_copy(w_hbm, w, ls.at[CH])
    my_heads = cols(core * 256, 256)
    k_copy = pltpu.make_async_copy(k_hbm.at[:, my_heads], kb.at[rows(s * 128, 128), :], ls.at[CH + 1])
    v_copy = pltpu.make_async_copy(v_hbm.at[:, my_heads], vb.at[rows(s * 128, 128), :], ls.at[CH + 2])
    q_copy = pltpu.make_async_copy(q_hbm.at[:, my_heads], q2.at[rows(core * TOK, TOK), :], ls.at[CH + 3])
    m_copy = pltpu.make_async_copy(mask_ref, mask2.at[:, cols(core * TOK, TOK)], ls.at[CH + 4])
    for c in (w_copy, k_copy, v_copy, q_copy, m_copy):
        c.start()

    pl.semaphore_wait(barrier, 18)

    def stage_a(i):
        copy(AGY, i, cot_hbm.at[:, cols(chunk(i) * WC, WC)], cot.at[i, rows(t * 64, 64), :], par).start()

    stage_a(0)
    stage_a(1)

    def extra(n, src, dst):
        return pltpu.make_async_remote_copy(
            src_ref=src, dst_ref=dst, send_sem=es.at[n], recv_sem=er.at[n], device_id=sib, device_id_type=MESH
        )

    other_heads = cols((1 - core) * 256, 256)
    q_send = extra(0, q_hbm.at[:, other_heads], q2.at[rows(core * TOK, TOK), :])
    q_send.start()
    m_send = extra(1, mask_ref, mask2.at[:, cols(core * TOK, TOK)])
    m_send.start()

    def kv_copies(j, dst_rows):
        d = (s + j) % 16
        heads = cols((d % 2) * 256, 256)
        return (
            pltpu.make_async_remote_copy(
                src_ref=k_hbm.at[:, heads], dst_ref=kb.at[dst_rows, :], send_sem=ks.at[j], recv_sem=kr.at[j],
                device_id=(d, t), device_id_type=MESH),
            pltpu.make_async_remote_copy(
                src_ref=v_hbm.at[:, heads], dst_ref=vb.at[dst_rows, :], send_sem=vs.at[j], recv_sem=vr.at[j],
                device_id=(d, t), device_id_type=MESH),
        )

    def kv_start(j, c):
        for copy_ in kv_copies(j, rows(s * 128, 128)):
            copy_.start()
        return c

    lax.fori_loop(1, 16, kv_start, 0)

    gate = jnp.tanh(gate_ref[...])

    def stage_b(i):
        own_piece(i).wait()
        got(AGY, i, cot.at[i, rows((x * 2 + 1 - yh) * 64, 64), :])
        block = cot.at[i, rows(x * 128, 128), :]
        copy(AGP, i, block, block, nxt).start()
        copy(AGM, i, block, block, prv).start()

    def stage_c(i):
        got(AGP, i, cot.at[i, rows(xb * 128, 128), :])
        top = cot.at[i, rows(xb * 128, 64), :]
        copy(AFP, i, top, top, nxt).start()
        got(AGM, i, cot.at[i, rows(xn * 128, 128), :])
        low = cot.at[i, rows(xn * 128 + 64, 64), :]
        copy(AFM, i, low, low, prv).start()

    def stage_d(i):
        got(AFP, i, cot.at[i, rows(xf * 128, 64), :])
        got(AFM, i, cot.at[i, rows(xf * 128 + 64, 64), :])
        copy(SIB, i, cot.at[i, :, cols((1 - core) * HALF, HALF)], cot_sib.at[i], sib).start()

    def stage_e(i):
        cc = cols(chunk(i) * WC, WC)
        for part in range(2):
            rr = pl.ds(part * 256, 256)
            gh_acc[rr, :] += dot(w[rr, cc], cot[i], NT)

    def stage_f(i):
        got(SIB, i, cot_sib.at[i])
        mine = cols(core * TOK, TOK)
        theirs = cols((1 - core) * TOK, TOK)
        for part in range(2):
            rr = pl.ds(part * 256, 256)
            val = dot(ht[rr, mine], cot[i, :, cols(core * HALF, HALF)], NN) + dot(ht[rr, theirs], cot_sib[i], NN)
            gw_out[i, rr, :] = val.astype(BF)

        @pl.when(i > 0)
        def _():
            copy(GW, i, gw_out.at[i], gw_in.at[i - 1], (chunk(i) * 2 + core, t)).start()

    def stage_la(i):
        block = cot.at[i, rows(x * 128, 128), :]
        half = cot.at[i, rows(x * 128, 64), :]
        sent(AGP, i, block)
        sent(AGM, i, block)
        sent(AFP, i, half)
        sent(AFM, i, half)
        sent(SIB, i, cot_sib.at[i])
        for part in range(2):
            cc = cols(chunk(i) * WC + part * HALF, HALF)
            cot[i, :, pl.ds(part * HALF, HALF)] = dot(hrow[...], w[:, cc], NN).astype(BF)
        copy(F1, i, cot.at[i, rows(xf * 128, 64), :], f1b.at[i], nxt).start()
        copy(F2, i, cot.at[i, rows(xf * 128 + 64, 64), :], f2b.at[i], prv).start()

    def stage_lb(i):
        got(F1, i, f1b.at[i])
        rr = rows(xn * 128, 64)
        cot[i, rr, :] = (cot[i, rr, :].astype(F32) + f1b[i].astype(F32)).astype(BF)
        copy(R1, i, cot.at[i, rows(xn * 128, 128), :], r1b.at[i], nxt).start()
        got(F2, i, f2b.at[i])
        rr = rows(xb * 128 + 64, 64)
        cot[i, rr, :] = (cot[i, rr, :].astype(F32) + f2b[i].astype(F32)).astype(BF)
        copy(R2, i, cot.at[i, rows(xb * 128, 128), :], r2b.at[i], prv).start()

    def reduced(i, which):
        rr = rows(which * 64, 64)
        return (
            cot[i, rows(x * 128 + which * 64, 64), :].astype(F32)
            + r1b[i, rr, :].astype(F32)
            + r2b[i, rr, :].astype(F32)
        )

    def stage_lc(i):
        got(R1, i, r1b.at[i])
        got(R2, i, r2b.at[i])
        ys[i] = reduced(i, 1 - yh).astype(BF)
        copy(YX, i, ys.at[i], yr.at[i], par).start()

    def stage_ld(i):
        got(YX, i, yr.at[i])
        total = reduced(i, yh) + yr[i].astype(F32)
        layer_ref[:, cols(chunk(i) * WC, WC)] = (gate * total).astype(BF)

    def masked(score, row, tok):
        return jnp.where(mask2[pl.ds(row, 1), tok] > 0, score, NEG)

    def forward(j):
        hh, u = j // 2, j % 2
        hc = cols(hh * HD, HD)
        tok = cols(u * TOK, TOK)
        qv = q2[rows(u * TOK, TOK), hc]

        def scores(ab, best):
            part = dot(kb[rows(ab * 256, 256), hc], qv, NT)
            for b in range(2):
                val = masked(part[b * 128 : (b + 1) * 128], ab * 2 + b, tok)
                sc[rows(ab * 256 + b * 128, 128), :] = val
                best = jnp.maximum(best, jnp.max(val, axis=0, keepdims=True))
            return best

        best = lax.fori_loop(0, AUD // 256, scores, jnp.full((1, TOK), NEG, F32))

        def weigh(ab, total):
            rr = rows(ab * 256, 256)
            val = jnp.exp2((sc[rr, :] - best) * C2)
            pb[rr, :] = val.astype(BF)
            return total + jnp.sum(val, axis=0, keepdims=True)

        total = lax.fori_loop(0, AUD // 256, weigh, jnp.zeros((1, TOK), F32))
        out = dot(vb[:, hc], pb[...], TN)
        ht[rows(core * 256 + hh * HD, HD), tok] = (out / total).astype(BF)
        lse[hh, :, tok] = best * C2 + jnp.log2(total)

    def kv_send(hh, d):
        return pltpu.make_async_remote_copy(
            src_ref=kv_out.at[hh, rows(d * 128, 128), :], dst_ref=kv_in.at[hh, (d - s + 16) % 16],
            send_sem=ds_.at[hh, (d - s + 16) % 16], recv_sem=dr.at[hh, (d - s + 16) % 16],
            device_id=(d, t), device_id_type=MESH,
        )

    def backward(j):
        hh = j // 2
        ah = (j + chip // 4) % 2
        hc = cols(hh * HD, HD)
        hr = rows(hh * HD, HD)
        first = j % 2 == 0

        @pl.when(first)
        def _():
            dq_acc[...] = jnp.zeros_like(dq_acc)
            own = ht[rows(core * 256 + hh * HD, HD), :].astype(F32)
            delta[...] = jnp.sum(gh2[hr, :].astype(F32) * own, axis=0, keepdims=True)

        def step(b, c):
            rr = rows(ah * 1024 + b * 256, 256)
            kk = kb[rr, hc]
            vv = vb[rr, hc]
            qv = q2[:, hc]
            gv = gh2[hr, :]
            score = dot(kk, qv, NT)
            logs = lse[hh]
            probs = []
            for m in range(2):
                row = ah * 8 + b * 2 + m
                val = masked(score[m * 128 : (m + 1) * 128], row, slice(None))
                probs.append(jnp.exp2(val * C2 - logs))
            prob = jnp.concatenate(probs, axis=0)
            dp = dot(vv, gv, NN)
            dsc = (prob * (dp - delta[...])).astype(BF)
            kv_out[hh, rr, pl.ds(HD, HD)] = dot(prob.astype(BF), gv, NT).astype(BF)
            kv_out[hh, rr, pl.ds(0, HD)] = (SCALE * dot(dsc, qv, NN)).astype(BF)
            dq_acc[...] += dot(kk, dsc, TN)
            return c

        lax.fori_loop(0, 4, step, 0)

        def send(d, c):
            @pl.when(ah * 8 + d != s)
            def _():
                kv_send(hh, ah * 8 + d).start()

            return c

        lax.fori_loop(0, 8, send, 0)

        @pl.when(j % 2 == 1)
        def _():
            full = SCALE * dq_acc[...]
            for u in range(2):
                piece = full[:, u * TOK : (u + 1) * TOK].T.astype(BF)

                @pl.when(core == u)
                def _():
                    dq_ref[:, cols(core * 256 + hh * HD, HD)] = piece

                @pl.when(core != u)
                def _():
                    dq_out[:, hc] = piece

    mine_rows = rows(core * 256, 256)
    ht_send = extra(2, ht.at[mine_rows, :], ht.at[mine_rows, :])
    their_rows = rows((1 - core) * 256, 256)
    gh_send = extra(3, gh_own.at[their_rows, :], gh2.at[:, cols(core * TOK, TOK)])
    dq_send = extra(4, dq_out, dq_in)

    gh_acc[...] = jnp.zeros_like(gh_acc)
    w_copy.wait()

    def f_low(g):
        return jnp.minimum(2 * (g - 5), g - 2)

    def tick(g, c):
        def stage(low, n, fn, idx):
            @pl.when((g >= low) & (g < low + n))
            def _():
                fn(idx)

        stage(0, CH - 2, stage_a, g + 2)
        stage(0, CH, stage_b, g)
        stage(1, CH, stage_c, g - 1)
        stage(2, CH, stage_d, g - 2)
        stage(6, CH, stage_lb, g - 6)
        stage(7, CH, stage_lc, g - 7)
        stage(8, CH, stage_ld, g - 8)
        stage(2, CH, stage_e, g - 2)

        @pl.when(g == 3)
        def _():
            k_copy.wait()
            v_copy.wait()
            q_copy.wait()
            m_copy.wait()
            extra(0, q2.at[rows((1 - core) * TOK, TOK), :], q2.at[rows((1 - core) * TOK, TOK), :]).wait_recv()
            other = mask2.at[:, cols((1 - core) * TOK, TOK)]
            extra(1, other, other).wait_recv()

            def kv_got(j, c2):
                for copy_ in kv_copies(j, rows(((s - j + 16) % 16) * 128, 128)):
                    copy_.wait_recv()
                return c2

            lax.fori_loop(1, 16, kv_got, 0)

        @pl.when((g >= 3) & (g < 5))
        def _():
            def unit(j, c2):
                forward((g - 3) * 2 + j)
                return c2

            lax.fori_loop(0, 2, unit, 0)

        @pl.when(g == 4)
        def _():
            ht_send.start()

        @pl.when(g == 5)
        def _():
            extra(2, ht.at[their_rows, :], ht.at[their_rows, :]).wait_recv()
            hrow[...] = ht[:, cols(core * TOK, TOK)].astype(F32).T.astype(BF)

        @pl.when((g >= 5) & (g < 10))
        def _():
            def unit(i, c2):
                stage_f(i)
                return c2

            lax.fori_loop(f_low(g), f_low(g + 1), unit, 0)

        stage(5, CH, stage_la, g - 5)

        @pl.when(g == 9)
        def _():
            gh_own[...] = (gate * gh_acc[...]).astype(BF)
            gh2[:, cols(core * TOK, TOK)] = gh_own[mine_rows, :]
            gh_send.start()

        @pl.when(g == 10)
        def _():
            other = gh2.at[:, cols((1 - core) * TOK, TOK)]
            extra(3, other, other).wait_recv()

        stage(10, 4, backward, g - 10)

        @pl.when(g == 13)
        def _():
            dq_send.start()

        return c

    lax.fori_loop(0, 16, tick, 0)

    def gw_got(i, c):
        got(GW, i, gw_in.at[i - 1])
        return c

    lax.fori_loop(1, CH, gw_got, 0)

    def gw_sum(b, c):
        rr = rows(b * 64, 64)
        total = gw_out[0, rr, :].astype(F32)
        for i in range(CH - 1):
            total += gw_in[i, rr, :].astype(F32)
        gw_ref[rr, :] = (gate * total).astype(BF)
        return c

    lax.fori_loop(0, 8, gw_sum, 0)

    dq_send.wait_recv()
    dq_ref[:, cols((1 - core) * 256, 256)] = dq_in[...]

    def kv_got2(j, c):
        for hh in range(2):
            slot = kv_in.at[hh, j]
            pltpu.make_async_remote_copy(
                src_ref=slot, dst_ref=slot, send_sem=ds_.at[hh, j], recv_sem=dr.at[hh, j],
                device_id=sib, device_id_type=MESH,
            ).wait_recv()
        return c

    lax.fori_loop(1, 16, kv_got2, 0)
    for hh in range(2):
        same = kv_out[hh, rows(s * 128, 128), :].astype(F32)
        for j in range(2, 16, 2):
            same += kv_in[hh, j].astype(F32)
        other = kv_in[hh, 1].astype(F32)
        for j in range(3, 16, 2):
            other += kv_in[hh, j].astype(F32)
        hc = cols(core * 256 + hh * HD, HD)
        dk_ref[:, hc] = same[:, :HD].astype(BF)
        dv_ref[:, hc] = same[:, HD:].astype(BF)
        hc = cols((1 - core) * 256 + hh * HD, HD)
        dk_ref[:, hc] = other[:, :HD].astype(BF)
        dv_ref[:, hc] = other[:, HD:].astype(BF)

    def all_sent(i, c):
        sent(AGY, i, cot.at[i, rows(x * 128, 64), :])
        sent(F1, i, f1b.at[i])
        sent(F2, i, f2b.at[i])
        sent(R1, i, r1b.at[i])
        sent(R2, i, r2b.at[i])
        sent(YX, i, ys.at[i])

        @pl.when(i > 0)
        def _():
            sent(GW, i, gw_out.at[i])

        return c

    lax.fori_loop(0, CH, all_sent, 0)

    def kv_sent(j, c):
        for copy_ in kv_copies(j, rows(s * 128, 128)):
            copy_.wait_send()
        for hh in range(2):
            slot = kv_in.at[hh, j]
            pltpu.make_async_remote_copy(
                src_ref=slot, dst_ref=slot, send_sem=ds_.at[hh, j], recv_sem=dr.at[hh, j],
                device_id=sib, device_id_type=MESH,
            ).wait_send()
        return c

    lax.fori_loop(1, 16, kv_sent, 0)
    for c in (q_send, m_send, ht_send, gh_send, dq_send):
        c.wait_send()


def per_device(queries, audio_keys, audio_values, out_weight, mix_gate, block_mask, cotangent):
    mask_rows = jnp.repeat(block_mask.T.astype(F32), BLK, axis=1)
    hbm = pl.BlockSpec(memory_space=pl.ANY)
    vmem = pl.BlockSpec(memory_space=pltpu.VMEM)
    dma = pltpu.SemaphoreType.DMA
    return pl.pallas_call(
        kernel,
        out_shape=(
            jax.ShapeDtypeStruct((64, 8192), BF),
            jax.ShapeDtypeStruct((TOK, 512), BF),
            jax.ShapeDtypeStruct((128, 512), BF),
            jax.ShapeDtypeStruct((128, 512), BF),
            jax.ShapeDtypeStruct((512, 512), BF),
        ),
        in_specs=[hbm, hbm, hbm, hbm, vmem, vmem, hbm],
        out_specs=[vmem] * 5,
        scratch_shapes=[
            pltpu.VMEM((512, 8192), BF),
            pltpu.VMEM((CH, TOK, WC), BF),
            pltpu.VMEM((CH, TOK, HALF), BF),
            pltpu.VMEM((AUD, 256), BF),
            pltpu.VMEM((AUD, 256), BF),
            pltpu.VMEM((2 * TOK, 256), BF),
            pltpu.VMEM((16, 2 * TOK), F32),
            pltpu.VMEM((512, 2 * TOK), BF),
            pltpu.VMEM((TOK, 512), BF),
            pltpu.VMEM((512, TOK), F32),
            pltpu.VMEM((512, TOK), BF),
            pltpu.VMEM((256, 2 * TOK), BF),
            pltpu.VMEM((AUD, TOK), F32),
            pltpu.VMEM((AUD, TOK), BF),
            pltpu.VMEM((2, 1, 2 * TOK), F32),
            pltpu.VMEM((1, 2 * TOK), F32),
            pltpu.VMEM((HD, 2 * TOK), F32),
            pltpu.VMEM((TOK, 256), BF),
            pltpu.VMEM((TOK, 256), BF),
            pltpu.VMEM((CH, 64, WC), BF),
            pltpu.VMEM((CH, 64, WC), BF),
            pltpu.VMEM((CH, 128, WC), BF),
            pltpu.VMEM((CH, 128, WC), BF),
            pltpu.VMEM((CH, 64, WC), BF),
            pltpu.VMEM((CH, 64, WC), BF),
            pltpu.VMEM((CH, 512, HALF), BF),
            pltpu.VMEM((CH - 1, 512, HALF), BF),
            pltpu.VMEM((2, AUD, 256), BF),
            pltpu.VMEM((2, 16, 128, 256), BF),
            dma((12, CH)), dma((12, CH)),
            dma((16,)), dma((16,)), dma((16,)), dma((16,)),
            dma((2, 16)), dma((2, 16)),
            dma((5,)), dma((5,)),
            dma((CH + 5,)),
        ],
        compiler_params=pltpu.CompilerParams(
            collective_id=0, has_side_effects=True, vmem_limit_bytes=62 * 2**20
        ),
        cost_estimate=pl.CostEstimate(flops=20 * 10**9, bytes_accessed=16 * 2**20, transcendentals=8 * 2**20),
    )(queries, audio_keys, audio_values, out_weight, mix_gate.reshape(1, 1), mask_rows, cotangent)


def solution(mesh):
    in_specs = (
        P("seq", "tp"),
        P("seq", "tp"),
        P("seq", "tp"),
        P("tp", None),
        P(),
        P("seq", None),
        P(("seq", "tp"), None),
    )
    out_specs = (
        P(("seq", "tp"), None),
        P("seq", "tp"),
        P("seq", "tp"),
        P("seq", "tp"),
        P("tp", "seq"),
    )
    return jax.shard_map(
        per_device, mesh=mesh, in_specs=in_specs, out_specs=out_specs, check_vma=False
    )
```

time: 544 us -> 195 us (0.36)
  waiting for transfers between devices: 415 us -> 0 us
  Pallas kernels: 0 us -> 180 us
  matrix products: 74.6 us -> 0 us
  local copies, waits for them, and re-layouts: 24.3 us -> 9.92 us
  between operations: 14.9 us -> 1.29 us
  other arithmetic: 12.5 us -> 0.68 us
    reduce_scatter x3 -> x0, waiting for transfers between devices: 249 us -> none  [the longest x1 118 us: per_device(): lax.psum_scatter(jnp.dot(heads_out, out_weight, preferred_element_type=jn...]
    pallas_call x0 -> x1, Pallas kernels: none -> 180 us  [per_device(): pl.pallas_call(kernel, out_shape=(jax.ShapeDtypeStruct((64, 8192), BF), j...]
    all_gather x3 -> x0, waiting for transfers between devices: 165 us -> none  [the longest x1 98.8 us: per_device(): full_grad = lax.all_gather(cotangent, 'tp', axis=0, tiled=True)]
    dot_general x9 -> x0, matrix products: 74.6 us -> none  [the longest x1 12.4 us: per_device(): jnp.einsum('thd,ahd->hta', grad_heads3, value_heads, preferred_element_ty...]
    reshape x3 -> x0, local copies, waits for them, and re-layouts: 8.1 us -> none  [the longest x1 3.99 us: per_device(): value_term.reshape(span_rows, feature_count)]
  transfers between devices with their start and end apart: 6 -> 0, of which waited for: 6 -> 0; matrix products, arithmetic and copies ran while one was open for 10% -> 0% of each run, Pallas kernels for 0% -> 0%
where the time goes in v1:
time: 195 us; the launch traced here: 192 us
  Pallas kernels  180 us (92%)
  local copies, waits for them, and re-layouts  9.92 us (5%)
    pallas_call x1, Pallas kernels, per_device(): pl.pallas_call(kernel, out_shape=(jax.ShapeDtypeStruct((64, 8192), BF), j...  180 us
    unnamed x6, local copies, waits for them, and re-layouts  9.76 us

profile of v1, /device:TPU:1, one launch (start us, length us, event | category | flops | bytes accessed | tf_op | source)
XLA Modules:
  0.0 192.1 jit_solution(5250558190199584195)
XLA Ops:
  1.3 0.7 convert_bitcast_fusion
  2.0 0.1 copy.12
  2.0 0.1 broadcast_in_dim.3
  2.1 0.6 copy.15
  2.8 180.2 %shard_map.110 = (bf16[64,8192]{1,0:T(8,128)(2,1)}, bf16[512,512]{1,0:T(8,128)(2,1)}, bf16[128,512]{1,0:T(8,128)(2,1)}, bf16[128,512]{1,0:T(8,128)(2,1)}, bf16[512,512]{1,0:T(8,128)(2,1)}) custom-call(bf16[512,512]{1,0:T(8,128)(2,1)} %q_hbm.1, bf16[128,512]{1,0:T(8,128)(2,1)} %k_hbm.1, bf16[128,512]{1,0:T(8,128)(2,1)} %v_hbm.1, bf16[512,8192]{1,0:T(8,128)(2,1)} %w_hbm.1, ...), custom_call_target="tpu_custom_call" | custom-call | flops 20000000000 | bytes 16777216 | tf_op jit(solution)/shard_map/pallas_call | solution.py:492
  183.0 2.3 %copy.22 = bf16[64,8192]{1,0:T(8,128)(2,1)} copy(bf16[64,8192]{1,0:T(8,128)(2,1)} %get-tuple-element.10) | data formatting | bytes 2097152
  185.2 1.9 copy.23
  187.1 1.6 copy.24
  188.6 1.6 copy.25
  190.2 1.9 copy.26

commit v2 on v1

v2 whole, which is shorter than its diff:
```python
import jax
import jax.numpy as jnp
from jax import lax
from jax.experimental import pallas as pl
from jax.experimental.pallas import tpu as pltpu
from jax.sharding import PartitionSpec as P

HD = 128
BLK = 128
CH = 8
WC = 1024
HALF = 512
TOK = 512
AUD = 2048
SCALE = HD ** (-0.5)
C2 = SCALE * 1.4426950408889634
NEG = -1e30
BF = jnp.bfloat16
F32 = jnp.float32
MESH = pl.DeviceIdType.MESH

NT = (((1,), (1,)), ((), ()))
NN = (((1,), (0,)), ((), ()))
TN = (((0,), (0,)), ((), ()))

AGY, AGP, AGM, AFP, AFM, SIB, GW, F1, F2, R1, R2, YX, YP, YM, YF, P0 = range(16)
KINDS = P0 + 4
GATHER_X = (0, 3, 5)
SCATTER_Y = (2, 4, 6)


def dot(a, b, dims):
    return lax.dot_general(a, b, dims, preferred_element_type=F32)


def kernel(
    q_hbm, k_hbm, v_hbm, w_hbm, gate_ref, mask_ref, cot_hbm,
    layer_ref, dq_ref, dk_ref, dv_ref, gw_ref,
    w, cot, cot_sib, kvb, q2, mask2, ht, hrow, gh_acc, gh_own, gh2,
    sc, pb, lse, delta, dq_acc, dq_out, dq_in, f1b, f2b, r1b, r2b, ys, yr, p4b, gw_out, gw_in, gw_sum, gw_par, kv_out, kv_in, kv_red, kv_fin,
    ss, rs, ps, pr, zs, zr, ds_, dr, fs, fr, es, er, ls,
):
    s = lax.axis_index("seq")
    t = lax.axis_index("tp")
    core = s % 2
    z = s // 4
    yl = (s // 2) % 2
    x = t // 2
    yh = t % 2
    xn, xb, xf = (x + 1) % 4, (x + 3) % 4, (x + 2) % 4
    sib = (s + 1 - 2 * core, t)
    nxt = (s, xn * 2 + yh)
    prv = (s, xb * 2 + yh)
    par = (s, x * 2 + 1 - yh)

    def zdev(dz):
        return (((z + dz) % 4) * 4 + yl * 2 + core, t)

    def near(n):
        return (z * 4 + ((yl + n // 2) % 2) * 2 + (core + n) % 2, t)

    def rows(start, size):
        return pl.ds(pl.multiple_of(start, size), size)

    def cols(start, size):
        return pl.ds(pl.multiple_of(start, 128), size)

    def chunk(i):
        m = i // 2
        zz = ((z // 2 + m // 2) % 2) * 2 + (z + m) % 2
        return zz * 2 + (yl + i) % 2

    def copy(kind, i, src, dst, dev):
        return pltpu.make_async_remote_copy(
            src_ref=src, dst_ref=dst, send_sem=ss.at[kind, i], recv_sem=rs.at[kind, i],
            device_id=dev, device_id_type=MESH,
        )

    def got(kind, i, dst):
        copy(kind, i, dst, dst, nxt).wait_recv()

    def sent(kind, i, src):
        copy(kind, i, src, src, nxt).wait_send()

    barrier = pltpu.get_barrier_semaphore()
    for dev in (nxt, prv, par):
        pl.semaphore_signal(barrier, inc=1, device_id=dev, device_id_type=MESH)

    for n in range(1, 4):
        pl.semaphore_signal(barrier, inc=1, device_id=near(n), device_id_type=MESH)
        pl.semaphore_signal(barrier, inc=1, device_id=zdev(n), device_id_type=MESH)

    def own_piece(i):
        return pltpu.make_async_copy(
            cot_hbm.at[:, cols(chunk(i) * WC, WC)], cot.at[i, rows(t * 64, 64), :], ls.at[i]
        )

    def start_piece(i, c):
        own_piece(i).start()
        return c

    lax.fori_loop(0, CH, start_piece, 0)
    w_copy = pltpu.make_async_copy(w_hbm, w, ls.at[CH])
    my_heads = cols(core * 256, 256)
    k_copy = pltpu.make_async_copy(k_hbm.at[:, my_heads], kvb.at[rows(s * 128, 128), pl.ds(0, 256)], ls.at[CH + 1])
    v_copy = pltpu.make_async_copy(v_hbm.at[:, my_heads], kvb.at[rows(s * 128, 128), pl.ds(256, 256)], ls.at[CH + 2])
    q_copy = pltpu.make_async_copy(q_hbm.at[:, my_heads], q2.at[rows(core * TOK, TOK), :], ls.at[CH + 3])
    m_copy = pltpu.make_async_copy(mask_ref, mask2.at[:, cols(core * TOK, TOK)], ls.at[CH + 4])
    for c in (w_copy, k_copy, v_copy, q_copy, m_copy):
        c.start()

    pl.semaphore_wait(barrier, 9)

    def stage_a(i):
        copy(AGY, i, cot_hbm.at[:, cols(chunk(i) * WC, WC)], cot.at[i, rows(t * 64, 64), :], par).start()

    def piece_x(i):
        src = cot_hbm.at[:, cols(chunk(i) * WC, WC)]
        dst = cot.at[i, rows(t * 64, 64), :]
        copy(AGP, i, src, dst, nxt).start()
        copy(AGM, i, src, dst, prv).start()

    piece_x(0)
    stage_a(1)

    def extra(n, src, dst):
        return pltpu.make_async_remote_copy(
            src_ref=src, dst_ref=dst, send_sem=es.at[n], recv_sem=er.at[n], device_id=sib, device_id_type=MESH
        )

    other_heads = cols((1 - core) * 256, 256)
    q_send = extra(0, q_hbm.at[:, other_heads], q2.at[rows(core * TOK, TOK), :])
    q_send.start()
    m_send = extra(1, mask_ref, mask2.at[:, cols(core * TOK, TOK)])
    m_send.start()

    def kv_near(n, src_rows):
        heads = cols(((core + n) % 2) * 256, 256)
        return [
            pltpu.make_async_remote_copy(
                src_ref=src.at[:, heads], dst_ref=kvb.at[src_rows, pl.ds(part * 256, 256)],
                send_sem=ps.at[n, part], recv_sem=pr.at[n, part], device_id=near(n), device_id_type=MESH)
            for part, src in enumerate((k_hbm, v_hbm))
        ]

    def kv_far(dz, zz):
        block = kvb.at[rows(zz * 512, 512), :]
        return pltpu.make_async_remote_copy(
            src_ref=block, dst_ref=block, send_sem=zs.at[dz], recv_sem=zr.at[dz],
            device_id=zdev(dz), device_id_type=MESH)

    for n in range(1, 4):
        for copy_ in kv_near(n, rows(s * 128, 128)):
            copy_.start()
    stage_a(2)
    stage_a(0)

    def kv_spread():
        k_copy.wait()
        v_copy.wait()
        for n in range(1, 4):
            src = z * 4 + ((yl + n // 2) % 2) * 2 + (core + n) % 2
            for copy_ in kv_near(n, rows(src * 128, 128)):
                copy_.wait_recv()
        for dz in (1, 3, 2):
            kv_far(dz, z).start()

    gate = jnp.tanh(gate_ref[...])

    def stage_b1(i):
        own_piece(i).wait()
        got(AGY, i, cot.at[i, rows((x * 2 + 1 - yh) * 64, 64), :])
        block = cot.at[i, rows(x * 128, 128), :]
        copy(AGP, i, block, block, nxt).start()
        copy(AGM, i, block, block, prv).start()

    def stage_c1(i):
        got(AGP, i, cot.at[i, rows(xb * 128, 128), :])
        top = cot.at[i, rows(xb * 128, 64), :]
        copy(AFP, i, top, top, nxt).start()
        got(AGM, i, cot.at[i, rows(xn * 128, 128), :])
        low = cot.at[i, rows(xn * 128 + 64, 64), :]
        copy(AFM, i, low, low, prv).start()

    def stage_d1(i):
        got(AFP, i, cot.at[i, rows(xf * 128, 64), :])
        got(AFM, i, cot.at[i, rows(xf * 128 + 64, 64), :])
        share(i)

    def share(i):
        copy(SIB, i, cot.at[i, :, cols((1 - core) * HALF, HALF)], cot_sib.at[i], sib).start()

    def to_partner(kind, i, xx):
        block = cot.at[i, rows(xx * 128 + yh * 64, 64), :]
        copy(kind, i, block, block, par).start()

    def stage_c2(i):
        got(AGP, i, cot.at[i, rows(xb * 128 + yh * 64, 64), :])
        top = cot.at[i, rows(xb * 128 + yh * 64, 32), :]
        copy(AFP, i, top, top, nxt).start()
        got(AGM, i, cot.at[i, rows(xn * 128 + yh * 64, 64), :])
        low = cot.at[i, rows(xn * 128 + yh * 64 + 32, 32), :]
        copy(AFM, i, low, low, prv).start()
        to_partner(YP, i, xb)
        to_partner(YM, i, xn)

    def stage_d2(i):
        got(AFP, i, cot.at[i, rows(xf * 128 + yh * 64, 32), :])
        got(AFM, i, cot.at[i, rows(xf * 128 + yh * 64 + 32, 32), :])
        to_partner(YF, i, xf)

    def stage_x2(i):
        own_piece(i).wait()
        for kind, xx in ((AGY, x), (YP, xb), (YM, xn), (YF, xf)):
            got(kind, i, cot.at[i, rows(xx * 128 + (1 - yh) * 64, 64), :])
        share(i)

    def either(first, second, cond):
        def stage(i):
            @pl.when(cond(i))
            def _():
                first(i)

            @pl.when(jnp.logical_not(cond(i)))
            def _():
                second(i)

        return stage

    def member(i, chosen):
        hit = i < 0
        for n in chosen:
            hit = jnp.logical_or(hit, i == n)
        return hit

    def gathers_x(i):
        return member(i, GATHER_X)

    stage_b = either(piece_x, stage_b1, gathers_x)
    stage_c = either(stage_c2, stage_c1, gathers_x)
    stage_d = either(stage_d2, stage_d1, gathers_x)

    def gather_sent(i):
        @pl.when(gathers_x(i))
        def _():
            for kind in (AGP, AGM, YP, YM, YF):
                sent(kind, i, cot.at[i, rows(x * 128, 64), :])
            for kind in (AFP, AFM):
                sent(kind, i, cot.at[i, rows(x * 128, 32), :])

        @pl.when(jnp.logical_not(gathers_x(i)))
        def _():
            for kind in (AGP, AGM):
                sent(kind, i, cot.at[i, rows(x * 128, 128), :])
            for kind in (AFP, AFM):
                sent(kind, i, cot.at[i, rows(x * 128, 64), :])

    def stage_e(i):
        cc = cols(chunk(i) * WC, WC)
        for part in range(2):
            rr = pl.ds(part * 256, 256)
            gh_acc[rr, :] += dot(w[rr, cc], cot[i], NT)

    def stage_f(i):
        got(SIB, i, cot_sib.at[i])
        mine = cols(core * TOK, TOK)
        theirs = cols((1 - core) * TOK, TOK)
        for part in range(2):
            rr = pl.ds(part * 256, 256)
            val = dot(ht[rr, mine], cot[i, :, cols(core * HALF, HALF)], NN) + dot(ht[rr, theirs], cot_sib[i], NN)
            gw_out[i, rr, :] = val.astype(BF)

        @pl.when(i > 1)
        def _():
            zz = chunk(i) // 2
            copy(GW, i, gw_out.at[i], gw_in.at[i - 2], (zz * 4 + yl * 2 + core, t)).start()

    def product(i):
        gather_sent(i)
        sent(SIB, i, cot_sib.at[i])
        for part in range(2):
            cc = cols(chunk(i) * WC + part * HALF, HALF)
            cot[i, :, pl.ds(part * HALF, HALF)] = dot(hrow[...], w[:, cc], NN).astype(BF)

    def stage_la1(i):
        product(i)
        copy(F1, i, cot.at[i, rows(xf * 128, 64), :], f1b.at[i], nxt).start()
        copy(F2, i, cot.at[i, rows(xf * 128 + 64, 64), :], f2b.at[i], prv).start()

    def stage_lb1(i):
        got(F1, i, f1b.at[i])
        rr = rows(xn * 128, 64)
        cot[i, rr, :] = (cot[i, rr, :].astype(F32) + f1b[i].astype(F32)).astype(BF)
        copy(R1, i, cot.at[i, rows(xn * 128, 128), :], r1b.at[i], nxt).start()
        got(F2, i, f2b.at[i])
        rr = rows(xb * 128 + 64, 64)
        cot[i, rr, :] = (cot[i, rr, :].astype(F32) + f2b[i].astype(F32)).astype(BF)
        copy(R2, i, cot.at[i, rows(xb * 128, 128), :], r2b.at[i], prv).start()

    def reduced(i, which):
        rr = rows(which * 64, 64)
        return (
            cot[i, rows(x * 128 + which * 64, 64), :].astype(F32)
            + r1b[i, rr, :].astype(F32)
            + r2b[i, rr, :].astype(F32)
        )

    def stage_lc1(i):
        got(R1, i, r1b.at[i])
        got(R2, i, r2b.at[i])
        ys[i] = reduced(i, 1 - yh).astype(BF)
        copy(YX, i, ys.at[i], yr.at[i], par).start()

    def stage_ld1(i):
        got(YX, i, yr.at[i])
        total = reduced(i, yh) + yr[i].astype(F32)
        layer_ref[:, cols(chunk(i) * WC, WC)] = (gate * total).astype(BF)

    def slot(i):
        return i // 2 - 1

    def stage_la2(i):
        product(i)
        for n in range(4):
            copy(P0 + n, i, cot.at[i, rows(n * 128 + (1 - yh) * 64, 64), :], p4b.at[slot(i), n], par).start()

    def add_partner(i, xx):
        rr = rows(xx * 128 + yh * 64, 64)
        return cot[i, rr, :].astype(F32) + p4b[slot(i), xx].astype(F32)

    def stage_lb2(i):
        for n in range(4):
            got(P0 + n, i, p4b.at[slot(i), n])
        rr = rows(xf * 128 + yh * 64, 64)
        cot[i, rr, :] = add_partner(i, xf).astype(BF)
        copy(F1, i, cot.at[i, rows(xf * 128 + yh * 64, 32), :], f1b.at[i, pl.ds(0, 32), :], nxt).start()
        copy(F2, i, cot.at[i, rows(xf * 128 + yh * 64 + 32, 32), :], f2b.at[i, pl.ds(0, 32), :], prv).start()

    def stage_lc2(i):
        top, low = pl.ds(0, 32), pl.ds(0, 64)
        got(F1, i, f1b.at[i, top, :])
        val = add_partner(i, xn)
        cot[i, rows(xn * 128 + yh * 64, 32), :] = (val[:32] + f1b[i, top, :].astype(F32)).astype(BF)
        cot[i, rows(xn * 128 + yh * 64 + 32, 32), :] = val[32:].astype(BF)
        copy(R1, i, cot.at[i, rows(xn * 128 + yh * 64, 64), :], r1b.at[i, low, :], nxt).start()
        got(F2, i, f2b.at[i, top, :])
        val = add_partner(i, xb)
        cot[i, rows(xb * 128 + yh * 64, 32), :] = val[:32].astype(BF)
        cot[i, rows(xb * 128 + yh * 64 + 32, 32), :] = (val[32:] + f2b[i, top, :].astype(F32)).astype(BF)
        copy(R2, i, cot.at[i, rows(xb * 128 + yh * 64, 64), :], r2b.at[i, low, :], prv).start()

    def stage_ld2(i):
        low = pl.ds(0, 64)
        got(R1, i, r1b.at[i, low, :])
        got(R2, i, r2b.at[i, low, :])
        total = add_partner(i, x) + r1b[i, low, :].astype(F32) + r2b[i, low, :].astype(F32)
        layer_ref[:, cols(chunk(i) * WC, WC)] = (gate * total).astype(BF)

    def scatters_y(i):
        return member(i, SCATTER_Y)

    stage_la = either(stage_la2, stage_la1, scatters_y)
    stage_lb = either(stage_lb2, stage_lb1, scatters_y)
    stage_lc = either(stage_lc2, stage_lc1, scatters_y)
    stage_ld = either(stage_ld2, stage_ld1, scatters_y)

    def masked(score, row, tok):
        return jnp.where(mask2[pl.ds(row, 1), tok] > 0, score, NEG)

    def forward(j):
        hh, u = j // 2, j % 2
        hc = cols(hh * HD, HD)
        vc = cols(256 + hh * HD, HD)
        tok = cols(u * TOK, TOK)
        qv = q2[rows(u * TOK, TOK), hc]

        def scores(ab, best):
            part = dot(kvb[rows(ab * 256, 256), hc], qv, NT)
            for b in range(2):
                val = masked(part[b * 128 : (b + 1) * 128], ab * 2 + b, tok)
                sc[rows(ab * 256 + b * 128, 128), :] = val
                best = jnp.maximum(best, jnp.max(val, axis=0, keepdims=True))
            return best

        best = lax.fori_loop(0, AUD // 256, scores, jnp.full((1, TOK), NEG, F32))

        def weigh(ab, total):
            rr = rows(ab * 256, 256)
            val = jnp.exp2((sc[rr, :] - best) * C2)
            pb[rr, :] = val.astype(BF)
            return total + jnp.sum(val, axis=0, keepdims=True)

        total = lax.fori_loop(0, AUD // 256, weigh, jnp.zeros((1, TOK), F32))
        out = dot(kvb[:, vc], pb[...], TN)
        ht[rows(core * 256 + hh * HD, HD), tok] = (out / total).astype(BF)
        lse[hh, :, tok] = best * C2 + jnp.log2(total)

    def kv_z(hh, dz):
        return pltpu.make_async_remote_copy(
            src_ref=kv_out.at[hh, rows(((z + dz) % 4) * 512, 512), :], dst_ref=kv_in.at[hh, dz - 1],
            send_sem=ds_.at[hh, dz], recv_sem=dr.at[hh, dz], device_id=zdev(dz), device_id_type=MESH)

    def kv_y(hh, n):
        src = ((yl + n // 2) % 2) * 2 + (core + n) % 2
        return pltpu.make_async_remote_copy(
            src_ref=kv_red.at[hh, src], dst_ref=kv_fin.at[hh, n],
            send_sem=fs.at[hh, n], recv_sem=fr.at[hh, n], device_id=near(n), device_id_type=MESH)

    def kv_reduce(hh):
        for dz in range(1, 4):
            kv_z(hh, dz).wait_recv()
        for b in range(4):
            total = kv_out[hh, rows(z * 512 + b * 128, 128), :].astype(F32)
            for dz in range(3):
                total += kv_in[hh, dz, b * 128 : (b + 1) * 128, :].astype(F32)
            kv_red[hh, b] = total.astype(BF)
        for n in range(1, 4):
            kv_y(hh, n).start()

    def kv_finish(hh):
        for n in range(1, 4):
            kv_y(hh, n).wait_recv()
        same = kv_red[hh, yl * 2 + core].astype(F32) + kv_fin[hh, 2].astype(F32)
        other = kv_fin[hh, 1].astype(F32) + kv_fin[hh, 3].astype(F32)
        hc = cols(core * 256 + hh * HD, HD)
        dk_ref[:, hc] = same[:, :HD].astype(BF)
        dv_ref[:, hc] = same[:, HD:].astype(BF)
        hc = cols((1 - core) * 256 + hh * HD, HD)
        dk_ref[:, hc] = other[:, :HD].astype(BF)
        dv_ref[:, hc] = other[:, HD:].astype(BF)

    gw_send = pltpu.make_async_remote_copy(
        src_ref=gw_sum, dst_ref=gw_par, send_sem=fs.at[0, 0], recv_sem=fr.at[0, 0],
        device_id=near(2), device_id_type=MESH)

    def gw_reduce(which, write):
        def got_one(i, c):
            got(GW, 2 * i + which, gw_in.at[2 * i + which - 2])
            return c

        lax.fori_loop(1, 4, got_one, 0)

        def add(b, c):
            rr = rows(b * 64, 64)
            total = gw_out[which, rr, :].astype(F32)
            for i in range(3):
                total += gw_in[2 * i + which, rr, :].astype(F32)
            write(rr, total)
            return c

        lax.fori_loop(0, 8, add, 0)

    def gw_part():
        def write(rr, total):
            gw_sum[rr, :] = total.astype(BF)

        gw_reduce(1, write)
        gw_send.start()

    def gw_finish():
        gw_send.wait_recv()

        def write(rr, total):
            gw_ref[rr, :] = (gate * (total + gw_par[rr, :].astype(F32))).astype(BF)

        gw_reduce(0, write)

    def backward(j):
        hh = j // 2
        ah = (j + 1 + z // 2) % 2
        hc = cols(hh * HD, HD)
        hr = rows(hh * HD, HD)
        first = j % 2 == 0

        @pl.when(first)
        def _():
            dq_acc[...] = jnp.zeros_like(dq_acc)
            own = ht[rows(core * 256 + hh * HD, HD), :].astype(F32)
            delta[...] = jnp.sum(gh2[hr, :].astype(F32) * own, axis=0, keepdims=True)

        def step(b, c):
            rr = rows(ah * 1024 + b * 256, 256)
            kk = kvb[rr, hc]
            vv = kvb[rr, cols(256 + hh * HD, HD)]
            qv = q2[:, hc]
            gv = gh2[hr, :]
            score = dot(kk, qv, NT)
            logs = lse[hh]
            probs = []
            for m in range(2):
                row = ah * 8 + b * 2 + m
                val = masked(score[m * 128 : (m + 1) * 128], row, slice(None))
                probs.append(jnp.exp2(val * C2 - logs))
            prob = jnp.concatenate(probs, axis=0)
            dp = dot(vv, gv, NN)
            dsc = (prob * (dp - delta[...])).astype(BF)
            kv_out[hh, rr, pl.ds(HD, HD)] = dot(prob.astype(BF), gv, NT).astype(BF)
            kv_out[hh, rr, pl.ds(0, HD)] = (SCALE * dot(dsc, qv, NN)).astype(BF)
            dq_acc[...] += dot(kk, dsc, TN)
            return c

        lax.fori_loop(0, 4, step, 0)

        for b in range(2):
            dz = (ah * 2 + b - z + 4) % 4

            @pl.when(dz > 0)
            def _():
                kv_z(hh, dz).start()

        @pl.when(j % 2 == 1)
        def _():
            full = SCALE * dq_acc[...]
            for u in range(2):
                piece = full[:, u * TOK : (u + 1) * TOK].T.astype(BF)

                @pl.when(core == u)
                def _():
                    dq_ref[:, cols(core * 256 + hh * HD, HD)] = piece

                @pl.when(core != u)
                def _():
                    dq_out[:, hc] = piece

    mine_rows = rows(core * 256, 256)
    ht_send = extra(2, ht.at[mine_rows, :], ht.at[mine_rows, :])
    their_rows = rows((1 - core) * 256, 256)
    gh_send = extra(3, gh_own.at[their_rows, :], gh2.at[:, cols(core * TOK, TOK)])
    dq_send = extra(4, dq_out, dq_in)

    gh_acc[...] = jnp.zeros_like(gh_acc)
    w_copy.wait()

    def tick(g, c):
        def stage(low, n, fn, idx):
            @pl.when((g >= low) & (g < low + n))
            def _():
                fn(idx)

        stage(0, CH - 3, stage_a, g + 3)
        stage(0, CH - 1, stage_b, g + 1)
        stage(0, CH, stage_c, g)

        @pl.when(g == 0)
        def _():
            kv_spread()

        stage(1, CH, stage_d, g - 1)

        def stage_ready(i):
            @pl.when(gathers_x(i))
            def _():
                stage_x2(i)
                stage_e(i)

        stage(3, CH, stage_ready, g - 3)

        def stage_ready1(i):
            @pl.when(jnp.logical_not(gathers_x(i)))
            def _():
                stage_e(i)

        stage(1, CH, stage_ready1, g - 1)

        @pl.when(g == 3)
        def _():
            q_copy.wait()
            m_copy.wait()
            extra(0, q2.at[rows((1 - core) * TOK, TOK), :], q2.at[rows((1 - core) * TOK, TOK), :]).wait_recv()
            other = mask2.at[:, cols((1 - core) * TOK, TOK)]
            extra(1, other, other).wait_recv()
            for dz in range(1, 4):
                kv_far(dz, (z - dz + 4) % 4).wait_recv()

        @pl.when((g >= 3) & (g < 5))
        def _():
            def unit(j, c2):
                forward((g - 3) * 2 + j)
                return c2

            lax.fori_loop(0, 2, unit, 0)

        @pl.when(g == 4)
        def _():
            ht_send.start()

        @pl.when(g == 5)
        def _():
            extra(2, ht.at[their_rows, :], ht.at[their_rows, :]).wait_recv()
            hrow[...] = ht[:, cols(core * TOK, TOK)].astype(F32).T.astype(BF)

        @pl.when((g >= 5) & (g < 9))
        def _():
            def unit(i, c2):
                ready = i + 1 + 2 * gathers_x(i).astype(jnp.int32)

                @pl.when(jnp.maximum(ready, 5) == g)
                def _():
                    stage_f(i)

                return c2

            lax.fori_loop(0, CH, unit, 0)

        @pl.when(g == 8)
        def _():
            gh_own[...] = (gate * gh_acc[...]).astype(BF)
            gh2[:, cols(core * TOK, TOK)] = gh_own[mine_rows, :]
            gh_send.start()

        stage(5, CH, stage_la, g - 5)
        stage(7, CH, stage_lb, g - 7)
        stage(8, CH, stage_lc, g - 8)
        stage(9, CH, stage_ld, g - 9)

        @pl.when(g == 9)
        def _():
            other = gh2.at[:, cols((1 - core) * TOK, TOK)]
            extra(3, other, other).wait_recv()

        stage(9, 4, backward, g - 9)

        @pl.when(g == 11)
        def _():
            gw_part()

        @pl.when(g == 12)
        def _():
            dq_send.start()
            kv_reduce(0)

        @pl.when(g == 13)
        def _():
            gw_finish()

        @pl.when(g == 14)
        def _():
            kv_reduce(1)
            kv_finish(0)

        return c

    lax.fori_loop(0, 17, tick, 0)

    dq_send.wait_recv()
    dq_ref[:, cols((1 - core) * 256, 256)] = dq_in[...]
    kv_finish(1)

    def all_sent(i, c):
        sent(AGY, i, cot.at[i, rows(x * 128, 64), :])

        @pl.when(scatters_y(i))
        def _():
            for n in range(4):
                sent(P0 + n, i, p4b.at[slot(i), n])
            for kind in (F1, F2):
                sent(kind, i, cot.at[i, rows(x * 128, 32), :])
            for kind in (R1, R2):
                sent(kind, i, cot.at[i, rows(x * 128, 64), :])

        @pl.when(jnp.logical_not(scatters_y(i)))
        def _():
            sent(F1, i, f1b.at[i])
            sent(F2, i, f2b.at[i])
            sent(R1, i, r1b.at[i])
            sent(R2, i, r2b.at[i])
            sent(YX, i, ys.at[i])

        @pl.when(i > 1)
        def _():
            sent(GW, i, gw_out.at[i])

        return c

    lax.fori_loop(0, CH, all_sent, 0)
    for n in range(1, 4):
        for copy_ in kv_near(n, rows(s * 128, 128)):
            copy_.wait_send()
        kv_far(n, z).wait_send()
        for hh in range(2):
            kv_z(hh, n).wait_send()
            kv_y(hh, n).wait_send()
    gw_send.wait_send()
    for c in (q_send, m_send, ht_send, gh_send, dq_send):
        c.wait_send()


def hand_over(*refs):
    sems = refs[10]
    copies = [pltpu.make_async_copy(refs[n], refs[5 + n], sems.at[n]) for n in range(5)]
    for c in copies:
        c.start()
    for c in copies:
        c.wait()


def per_device(queries, audio_keys, audio_values, out_weight, mix_gate, block_mask, cotangent):
    mask_rows = jnp.repeat(block_mask.T.astype(F32), BLK, axis=1)
    hbm = pl.BlockSpec(memory_space=pl.ANY)
    vmem = pl.BlockSpec(memory_space=pltpu.VMEM)
    dma = pltpu.SemaphoreType.DMA
    results = pl.pallas_call(
        kernel,
        out_shape=(
            jax.ShapeDtypeStruct((64, 8192), BF),
            jax.ShapeDtypeStruct((TOK, 512), BF),
            jax.ShapeDtypeStruct((128, 512), BF),
            jax.ShapeDtypeStruct((128, 512), BF),
            jax.ShapeDtypeStruct((512, 512), BF),
        ),
        in_specs=[hbm, hbm, hbm, hbm, vmem, vmem, hbm],
        out_specs=[vmem] * 5,
        scratch_shapes=[
            pltpu.VMEM((512, 8192), BF),
            pltpu.VMEM((CH, TOK, WC), BF),
            pltpu.VMEM((CH, TOK, HALF), BF),
            pltpu.VMEM((AUD, 512), BF),
            pltpu.VMEM((2 * TOK, 256), BF),
            pltpu.VMEM((16, 2 * TOK), F32),
            pltpu.VMEM((512, 2 * TOK), BF),
            pltpu.VMEM((TOK, 512), BF),
            pltpu.VMEM((512, TOK), F32),
            pltpu.VMEM((512, TOK), BF),
            pltpu.VMEM((256, 2 * TOK), BF),
            pltpu.VMEM((AUD, TOK), F32),
            pltpu.VMEM((AUD, TOK), BF),
            pltpu.VMEM((2, 1, 2 * TOK), F32),
            pltpu.VMEM((1, 2 * TOK), F32),
            pltpu.VMEM((HD, 2 * TOK), F32),
            pltpu.VMEM((TOK, 256), BF),
            pltpu.VMEM((TOK, 256), BF),
            pltpu.VMEM((CH, 64, WC), BF),
            pltpu.VMEM((CH, 64, WC), BF),
            pltpu.VMEM((CH, 128, WC), BF),
            pltpu.VMEM((CH, 128, WC), BF),
            pltpu.VMEM((CH, 64, WC), BF),
            pltpu.VMEM((CH, 64, WC), BF),
            pltpu.VMEM((3, 4, 64, WC), BF),
            pltpu.VMEM((CH, 512, HALF), BF),
            pltpu.VMEM((CH - 2, 512, HALF), BF),
            pltpu.VMEM((512, HALF), BF),
            pltpu.VMEM((512, HALF), BF),
            pltpu.VMEM((2, AUD, 256), BF),
            pltpu.VMEM((2, 3, 512, 256), BF),
            pltpu.VMEM((2, 4, 128, 256), BF),
            pltpu.VMEM((2, 4, 128, 256), BF),
            dma((KINDS, CH)), dma((KINDS, CH)),
            dma((4, 2)), dma((4, 2)),
            dma((4,)), dma((4,)),
            dma((2, 4)), dma((2, 4)),
            dma((2, 4)), dma((2, 4)),
            dma((5,)), dma((5,)),
            dma((CH + 5,)),
        ],
        compiler_params=pltpu.CompilerParams(
            collective_id=0, has_side_effects=True, vmem_limit_bytes=62 * 2**20
        ),
        cost_estimate=pl.CostEstimate(flops=20 * 10**9, bytes_accessed=16 * 2**20, transcendentals=8 * 2**20),
    )(queries, audio_keys, audio_values, out_weight, mix_gate.reshape(1, 1), mask_rows, cotangent)
    return pl.pallas_call(
        hand_over,
        out_shape=tuple(jax.ShapeDtypeStruct(r.shape, r.dtype) for r in results),
        in_specs=[vmem] * 5,
        out_specs=[hbm] * 5,
        scratch_shapes=[dma((5,))],
    )(*results)


def solution(mesh):
    in_specs = (
        P("seq", "tp"),
        P("seq", "tp"),
        P("seq", "tp"),
        P("tp", None),
        P(),
        P("seq", None),
        P(("seq", "tp"), None),
    )
    out_specs = (
        P(("seq", "tp"), None),
        P("seq", "tp"),
        P("seq", "tp"),
        P("seq", "tp"),
        P("tp", "seq"),
    )
    return jax.shard_map(
        per_device, mesh=mesh, in_specs=in_specs, out_specs=out_specs, check_vma=False
    )
```

time: 195 us -> 170 us (0.87)
  Pallas kernels: 180 us -> 164 us
  local copies, waits for them, and re-layouts: 9.92 us -> 0.79 us
    pallas_call x1, Pallas kernels: 180 us -> 161 us  [per_device(): pl.pallas_call(kernel, out_shape=(jax.ShapeDtypeStruct((64, 8192), BF), j...]
    unnamed x6 -> x1, local copies, waits for them, and re-layouts: 9.76 us -> 0.63 us
    pallas_call x0 -> x1, Pallas kernels: none -> 3.04 us  [per_device(): pl.pallas_call(hand_over, out_shape=tuple((jax.ShapeDtypeStruct(r.shape,...]
where the time goes in v2:
time: 170 us; the launch traced here: 167 us
  Pallas kernels  164 us (96%)
    pallas_call x1, Pallas kernels, per_device(): pl.pallas_call(kernel, out_shape=(jax.ShapeDtypeStruct((64, 8192), BF), j...  161 us

profile of v2, /device:TPU:1, one launch (start us, length us, event | category | flops | bytes accessed | tf_op | source)
XLA Modules:
  0.0 166.8 jit_solution(9086207772342517230)
XLA Ops:
  1.3 0.7 convert_bitcast_fusion
  2.0 0.1 copy.12
  2.0 0.1 broadcast_in_dim.3
  2.1 0.6 copy.15
  2.8 161.0 %shard_map.110 = (bf16[64,8192]{1,0:T(8,128)(2,1)}, bf16[512,512]{1,0:T(8,128)(2,1)}, bf16[128,512]{1,0:T(8,128)(2,1)}, bf16[128,512]{1,0:T(8,128)(2,1)}, bf16[512,512]{1,0:T(8,128)(2,1)}) custom-call(bf16[512,512]{1,0:T(8,128)(2,1)} %q_hbm.1, bf16[128,512]{1,0:T(8,128)(2,1)} %k_hbm.1, bf16[128,512]{1,0:T(8,128)(2,1)} %v_hbm.1, bf16[512,8192]{1,0:T(8,128)(2,1)} %w_hbm.1, ...), custom_call_target="tpu_custom_call" | custom-call | flops 20000000000 | bytes 16777216 | tf_op jit(solution)/shard_map/pallas_call | solution.py:702
  163.7 3.0 %shard_map.111 = (bf16[64,8192]{1,0:T(8,128)(2,1)}, bf16[512,512]{1,0:T(8,128)(2,1)}, bf16[128,512]{1,0:T(8,128)(2,1)}, bf16[128,512]{1,0:T(8,128)(2,1)}, bf16[512,512]{1,0:T(8,128)(2,1)}) custom-call(bf16[64,8192]{1,0:T(8,128)(2,1)} %get-tuple-element.10.refs_0_, bf16[512,512]{1,0:T(8,128)(2,1)} %get-tuple-element.11.refs_1_, ...), custom_call_target="tpu_custom_call" | custom-call | tf_op jit(solution)/shard_map/pallas_call | solution.py:760

commit v3 on v2

--- a/solution.py
+++ b/solution.py
@@ -25,8 +25,35 @@
 
 AGY, AGP, AGM, AFP, AFM, SIB, GW, F1, F2, R1, R2, YX, YP, YM, YF, P0 = range(16)
 KINDS = P0 + 4
-GATHER_X = (0, 3, 5)
-SCATTER_Y = (2, 4, 6)
+GATHER_X = (3, 5)
+SCATTER_Y = (1, 3, 5)
+TICKS = 48
+PLAN = (
+    ('BW', (31, 32, 33, 34), (0, 1, 2, 3)),
+    ('DQ', (38,), (0,)),
+    ('LB', (29, 30, 32, 34, 35, 38, 41, 42), (7, 5, 2, 0, 3, 1, 4, 6)),
+    ('LC', (35, 36, 37, 38, 39, 42, 45, 46), (5, 7, 2, 0, 3, 1, 4, 6)),
+    ('K0', (0,), (0,)),
+    ('GP', (36,), (0,)),
+    ('B', (0, 1, 10, 11, 12, 13, 14, 15), (3, 5, 4, 7, 1, 0, 2, 6)),
+    ('FW', (15, 16, 17, 18), (0, 1, 2, 3)),
+    ('A', (1, 2, 3, 4, 5, 6, 7, 8), (4, 5, 7, 1, 3, 0, 2, 6)),
+    ('C', (8, 9, 11, 12, 17, 20, 21, 22), (3, 5, 4, 7, 0, 2, 1, 6)),
+    ('K1', (8,), (0,)),
+    ('KR', (41, 45), (0, 1)),
+    ('D', (9, 10, 13, 17, 24, 25, 27, 28), (3, 5, 4, 7, 0, 2, 1, 6)),
+    ('HR', (21,), (0,)),
+    ('X', (18, 19), (3, 5)),
+    ('E', (13, 17, 18, 19, 24, 25, 27, 28), (4, 7, 3, 5, 0, 2, 1, 6)),
+    ('GH', (28,), (0,)),
+    ('F', (21, 23, 24, 25, 26, 28, 36, 37), (5, 7, 3, 0, 2, 1, 4, 6)),
+    ('KF', (45, 46), (0, 1)),
+    ('LD', (39, 40, 42, 43, 44, 45, 46, 47), (7, 5, 3, 2, 0, 4, 1, 6)),
+    ('DF', (38,), (0,)),
+    ('GF', (47,), (0,)),
+    ('LA', (22, 23, 24, 25, 26, 30, 36, 37), (5, 7, 3, 0, 2, 1, 4, 6)),
+    ('HX', (19,), (0,)),
+)
 
 
 def dot(a, b, dims):
@@ -120,8 +147,6 @@
         copy(AGP, i, src, dst, nxt).start()
         copy(AGM, i, src, dst, prv).start()
 
-    piece_x(0)
-    stage_a(1)
 
     def extra(n, src, dst):
         return pltpu.make_async_remote_copy(
@@ -149,11 +174,10 @@
             src_ref=block, dst_ref=block, send_sem=zs.at[dz], recv_sem=zr.at[dz],
             device_id=zdev(dz), device_id_type=MESH)
 
-    for n in range(1, 4):
-        for copy_ in kv_near(n, rows(s * 128, 128)):
-            copy_.start()
-    stage_a(2)
-    stage_a(0)
+    def kv_share():
+        for n in range(1, 4):
+            for copy_ in kv_near(n, rows(s * 128, 128)):
+                copy_.start()
 
     def kv_spread():
         k_copy.wait()
@@ -317,7 +341,7 @@
         layer_ref[:, cols(chunk(i) * WC, WC)] = (gate * total).astype(BF)
 
     def slot(i):
-        return i // 2 - 1
+        return sum((i > n).astype(jnp.int32) for n in SCATTER_Y)
 
     def stage_la2(i):
         product(i)
@@ -529,122 +553,87 @@
     dq_send = extra(4, dq_out, dq_in)
 
     gh_acc[...] = jnp.zeros_like(gh_acc)
-    w_copy.wait()
-
-    def tick(g, c):
-        def stage(low, n, fn, idx):
-            @pl.when((g >= low) & (g < low + n))
+
+    def heads_first():
+        q_copy.wait()
+        m_copy.wait()
+        other_q = q2.at[rows((1 - core) * TOK, TOK), :]
+        extra(0, other_q, other_q).wait_recv()
+        other_m = mask2.at[:, cols((1 - core) * TOK, TOK)]
+        extra(1, other_m, other_m).wait_recv()
+        for dz in range(1, 4):
+            kv_far(dz, (z - dz + 4) % 4).wait_recv()
+
+    def on_first(i, fn):
+        @pl.when(i == 0)
+        def _():
+            fn()
+
+    def stage_fw(j):
+        on_first(j, heads_first)
+        forward(j)
+
+    def gh_got():
+        other = gh2.at[:, cols((1 - core) * TOK, TOK)]
+        extra(3, other, other).wait_recv()
+
+    def stage_bw(j):
+        on_first(j, gh_got)
+        backward(j)
+
+    def stage_hr():
+        extra(2, ht.at[their_rows, :], ht.at[their_rows, :]).wait_recv()
+        hrow[...] = ht[:, cols(core * TOK, TOK)].astype(F32).T.astype(BF)
+
+    def stage_gh():
+        gh_own[...] = (gate * gh_acc[...]).astype(BF)
+        gh2[:, cols(core * TOK, TOK)] = gh_own[mine_rows, :]
+        gh_send.start()
+
+    def stage_df():
+        dq_send.wait_recv()
+        dq_ref[:, cols((1 - core) * 256, 256)] = dq_in[...]
+
+    once = {
+        "K0": kv_share, "K1": kv_spread, "HX": ht_send.start, "HR": stage_hr, "GH": stage_gh,
+        "GP": gw_part, "GF": gw_finish, "DQ": dq_send.start, "DF": stage_df,
+    }
+    each = {
+        "A": stage_a, "B": stage_b, "C": stage_c, "D": stage_d, "X": stage_x2, "E": stage_e, "F": stage_f,
+        "LA": stage_la, "LB": stage_lb, "LC": stage_lc, "LD": stage_ld,
+        "FW": stage_fw, "BW": stage_bw, "KR": kv_reduce, "KF": kv_finish,
+    }
+    w_tick = min(ticks[0] for name, ticks, _ in PLAN if name == "E")
+
+    def packed(ticks, low):
+        return jnp.int32(sum(1 << (n - low) for n in ticks if low <= n < low + 30))
+
+    def tick(g, state):
+        after = []
+        for (name, ticks, idx), (bits, order) in zip(PLAN, state):
+            for low in range(30, TICKS, 30):
+                bits = jnp.where(g == low, packed(ticks, low), bits)
+            hit = bits % 2 == 1
+            if name == "E":
+
+                @pl.when(g == w_tick)
+                def _():
+                    w_copy.wait()
+
+            @pl.when(hit)
             def _():
-                fn(idx)
-
-        stage(0, CH - 3, stage_a, g + 3)
-        stage(0, CH - 1, stage_b, g + 1)
-        stage(0, CH, stage_c, g)
-
-        @pl.when(g == 0)
-        def _():
-            kv_spread()
-
-        stage(1, CH, stage_d, g - 1)
-
-        def stage_ready(i):
-            @pl.when(gathers_x(i))
-            def _():
-                stage_x2(i)
-                stage_e(i)
-
-        stage(3, CH, stage_ready, g - 3)
-
-        def stage_ready1(i):
-            @pl.when(jnp.logical_not(gathers_x(i)))
-            def _():
-                stage_e(i)
-
-        stage(1, CH, stage_ready1, g - 1)
-
-        @pl.when(g == 3)
-        def _():
-            q_copy.wait()
-            m_copy.wait()
-            extra(0, q2.at[rows((1 - core) * TOK, TOK), :], q2.at[rows((1 - core) * TOK, TOK), :]).wait_recv()
-            other = mask2.at[:, cols((1 - core) * TOK, TOK)]
-            extra(1, other, other).wait_recv()
-            for dz in range(1, 4):
-                kv_far(dz, (z - dz + 4) % 4).wait_recv()
-
-        @pl.when((g >= 3) & (g < 5))
-        def _():
-            def unit(j, c2):
-                forward((g - 3) * 2 + j)
-                return c2
-
-            lax.fori_loop(0, 2, unit, 0)
-
-        @pl.when(g == 4)
-        def _():
-            ht_send.start()
-
-        @pl.when(g == 5)
-        def _():
-            extra(2, ht.at[their_rows, :], ht.at[their_rows, :]).wait_recv()
-            hrow[...] = ht[:, cols(core * TOK, TOK)].astype(F32).T.astype(BF)
-
-        @pl.when((g >= 5) & (g < 9))
-        def _():
-            def unit(i, c2):
-                ready = i + 1 + 2 * gathers_x(i).astype(jnp.int32)
-
-                @pl.when(jnp.maximum(ready, 5) == g)
-                def _():
-                    stage_f(i)
-
-                return c2
-
-            lax.fori_loop(0, CH, unit, 0)
-
-        @pl.when(g == 8)
-        def _():
-            gh_own[...] = (gate * gh_acc[...]).astype(BF)
-            gh2[:, cols(core * TOK, TOK)] = gh_own[mine_rows, :]
-            gh_send.start()
-
-        stage(5, CH, stage_la, g - 5)
-        stage(7, CH, stage_lb, g - 7)
-        stage(8, CH, stage_lc, g - 8)
-        stage(9, CH, stage_ld, g - 9)
-
-        @pl.when(g == 9)
-        def _():
-            other = gh2.at[:, cols((1 - core) * TOK, TOK)]
-            extra(3, other, other).wait_recv()
-
-        stage(9, 4, backward, g - 9)
-
-        @pl.when(g == 11)
-        def _():
-            gw_part()
-
-        @pl.when(g == 12)
-        def _():
-            dq_send.start()
-            kv_reduce(0)
-
-        @pl.when(g == 13)
-        def _():
-            gw_finish()
-
-        @pl.when(g == 14)
-        def _():
-            kv_reduce(1)
-            kv_finish(0)
-
-        return c
-
-    lax.fori_loop(0, 17, tick, 0)
-
-    dq_send.wait_recv()
-    dq_ref[:, cols((1 - core) * 256, 256)] = dq_in[...]
-    kv_finish(1)
+                if name in once:
+                    once[name]()
+                else:
+                    each[name](order % 8)
+
+            after.append((bits // 2, jnp.where(hit, order // 8, order)))
+        return tuple(after)
+
+    start = tuple(
+        (packed(ticks, 0), jnp.int32(sum(i << (3 * n) for n, i in enumerate(idx)))) for _, ticks, idx in PLAN
+    )
+    lax.fori_loop(0, TICKS, tick, start)
 
     def all_sent(i, c):
         sent(AGY, i, cot.at[i, rows(x * 128, 64), :])

time: 170 us -> 143 us (0.84); the launches traced: 167 us -> 143 us
  Pallas kernels: 164 us -> 140 us
    pallas_call x1, Pallas kernels: 161 us -> 137 us  [per_device(): pl.pallas_call(kernel, out_shape=(jax.ShapeDtypeStruct((64, 8192), BF), j...]
where the time goes in v3:
time: 143 us
  Pallas kernels  140 us (98%)
    pallas_call x1, Pallas kernels, per_device(): pl.pallas_call(kernel, out_shape=(jax.ShapeDtypeStruct((64, 8192), BF), j...  137 us
    pallas_call x1, Pallas kernels, per_device(): pl.pallas_call(hand_over, out_shape=tuple((jax.ShapeDtypeStruct(r.shape,...  3.04 us

profile of v3, /device:TPU:1, one launch (start us, length us, event | category | flops | bytes accessed | tf_op | source)
XLA Modules:
  0.0 142.6 jit_solution(16022930645918560487)
XLA Ops:
  1.3 0.7 convert_bitcast_fusion
  2.0 0.1 copy.12
  2.0 0.1 broadcast_in_dim.3
  2.1 0.6 copy.15
  2.8 136.8 %shard_map.110 = (bf16[64,8192]{1,0:T(8,128)(2,1)}, bf16[512,512]{1,0:T(8,128)(2,1)}, bf16[128,512]{1,0:T(8,128)(2,1)}, bf16[128,512]{1,0:T(8,128)(2,1)}, bf16[512,512]{1,0:T(8,128)(2,1)}) custom-call(bf16[512,512]{1,0:T(8,128)(2,1)} %q_hbm.1, bf16[128,512]{1,0:T(8,128)(2,1)} %k_hbm.1, bf16[128,512]{1,0:T(8,128)(2,1)} %v_hbm.1, bf16[512,8192]{1,0:T(8,128)(2,1)} %w_hbm.1, ...), custom_call_target="tpu_custom_call" | custom-call | flops 20000000000 | bytes 16777216 | tf_op jit(solution)/shard_map/pallas_call | solution.py:691
  139.6 3.0 %shard_map.111 = (bf16[64,8192]{1,0:T(8,128)(2,1)}, bf16[512,512]{1,0:T(8,128)(2,1)}, bf16[128,512]{1,0:T(8,128)(2,1)}, bf16[128,512]{1,0:T(8,128)(2,1)}, bf16[512,512]{1,0:T(8,128)(2,1)}) custom-call(bf16[64,8192]{1,0:T(8,128)(2,1)} %get-tuple-element.10.refs_0_, bf16[512,512]{1,0:T(8,128)(2,1)} %get-tuple-element.11.refs_1_, ...), custom_call_target="tpu_custom_call" | custom-call | tf_op jit(solution)/shard_map/pallas_call | solution.py:749

commit v4 on v3

--- a/solution.py
+++ b/solution.py
@@ -27,32 +27,33 @@
 KINDS = P0 + 4
 GATHER_X = (3, 5)
 SCATTER_Y = (1, 3, 5)
-TICKS = 48
+TICKS = 51
 PLAN = (
-    ('BW', (31, 32, 33, 34), (0, 1, 2, 3)),
-    ('DQ', (38,), (0,)),
-    ('LB', (29, 30, 32, 34, 35, 38, 41, 42), (7, 5, 2, 0, 3, 1, 4, 6)),
-    ('LC', (35, 36, 37, 38, 39, 42, 45, 46), (5, 7, 2, 0, 3, 1, 4, 6)),
+    ('HR', (18,), (0,)),
     ('K0', (0,), (0,)),
-    ('GP', (36,), (0,)),
-    ('B', (0, 1, 10, 11, 12, 13, 14, 15), (3, 5, 4, 7, 1, 0, 2, 6)),
-    ('FW', (15, 16, 17, 18), (0, 1, 2, 3)),
-    ('A', (1, 2, 3, 4, 5, 6, 7, 8), (4, 5, 7, 1, 3, 0, 2, 6)),
-    ('C', (8, 9, 11, 12, 17, 20, 21, 22), (3, 5, 4, 7, 0, 2, 1, 6)),
-    ('K1', (8,), (0,)),
-    ('KR', (41, 45), (0, 1)),
-    ('D', (9, 10, 13, 17, 24, 25, 27, 28), (3, 5, 4, 7, 0, 2, 1, 6)),
-    ('HR', (21,), (0,)),
-    ('X', (18, 19), (3, 5)),
-    ('E', (13, 17, 18, 19, 24, 25, 27, 28), (4, 7, 3, 5, 0, 2, 1, 6)),
-    ('GH', (28,), (0,)),
-    ('F', (21, 23, 24, 25, 26, 28, 36, 37), (5, 7, 3, 0, 2, 1, 4, 6)),
-    ('KF', (45, 46), (0, 1)),
-    ('LD', (39, 40, 42, 43, 44, 45, 46, 47), (7, 5, 3, 2, 0, 4, 1, 6)),
-    ('DF', (38,), (0,)),
-    ('GF', (47,), (0,)),
-    ('LA', (22, 23, 24, 25, 26, 30, 36, 37), (5, 7, 3, 0, 2, 1, 4, 6)),
-    ('HX', (19,), (0,)),
+    ('A', (0, 2, 3, 4, 5, 6, 9, 10), (4, 2, 0, 7, 1, 3, 5, 6)),
+    ('GP', (32,), (0,)),
+    ('F', (18, 19, 22, 24, 27, 29, 30, 36), (5, 7, 3, 2, 0, 6, 1, 4)),
+    ('GH', (29,), (0,)),
+    ('B', (0, 1, 7, 8, 9, 10, 11, 15), (3, 5, 4, 2, 7, 0, 1, 6)),
+    ('X', (15, 17), (5, 3)),
+    ('LC', (32, 36, 40, 41, 42, 43, 44, 45), (5, 7, 0, 2, 1, 6, 3, 4)),
+    ('E', (15, 19, 20, 22, 24, 25, 26, 28), (5, 7, 2, 3, 0, 4, 6, 1)),
+    ('LB', (30, 31, 32, 33, 36, 37, 38, 39), (5, 2, 7, 0, 3, 6, 1, 4)),
+    ('D', (9, 10, 15, 16, 20, 23, 25, 27), (5, 3, 2, 7, 4, 0, 6, 1)),
+    ('LA', (18, 22, 23, 25, 28, 29, 31, 36), (5, 7, 3, 2, 0, 6, 1, 4)),
+    ('KF', (45, 47), (1, 0)),
+    ('KR', (38, 44), (0, 1)),
+    ('K1', (6,), (0,)),
+    ('DQ', (39,), (0,)),
+    ('LD', (43, 44, 45, 46, 47, 48, 49, 50), (5, 0, 1, 6, 7, 2, 4, 3)),
+    ('C', (4, 6, 9, 10, 11, 16, 20, 21), (3, 5, 2, 7, 4, 0, 6, 1)),
+    ('GF', (50,), (0,)),
+    ('FW', (11, 12, 13, 14), (0, 1, 2, 3)),
+    ('HX', (14,), (0,)),
+    ('L0', (7,), (0,)),
+    ('DF', (42,), (0,)),
+    ('BW', (31, 33, 34, 35), (0, 1, 2, 3)),
 )
 
 
@@ -62,10 +63,11 @@
 
 def kernel(
     q_hbm, k_hbm, v_hbm, w_hbm, gate_ref, mask_ref, cot_hbm,
+    layer_hbm, dq_hbm, dk_hbm, dv_hbm, gw_hbm,
     layer_ref, dq_ref, dk_ref, dv_ref, gw_ref,
     w, cot, cot_sib, kvb, q2, mask2, ht, hrow, gh_acc, gh_own, gh2,
     sc, pb, lse, delta, dq_acc, dq_out, dq_in, f1b, f2b, r1b, r2b, ys, yr, p4b, gw_out, gw_in, gw_sum, gw_par, kv_out, kv_in, kv_red, kv_fin,
-    ss, rs, ps, pr, zs, zr, ds_, dr, fs, fr, es, er, ls,
+    ss, rs, ps, pr, zs, zr, ds_, dr, fs, fr, es, er, ls, os_,
 ):
     s = lax.axis_index("seq")
     t = lax.axis_index("tp")
@@ -132,11 +134,22 @@
     k_copy = pltpu.make_async_copy(k_hbm.at[:, my_heads], kvb.at[rows(s * 128, 128), pl.ds(0, 256)], ls.at[CH + 1])
     v_copy = pltpu.make_async_copy(v_hbm.at[:, my_heads], kvb.at[rows(s * 128, 128), pl.ds(256, 256)], ls.at[CH + 2])
     q_copy = pltpu.make_async_copy(q_hbm.at[:, my_heads], q2.at[rows(core * TOK, TOK), :], ls.at[CH + 3])
-    m_copy = pltpu.make_async_copy(mask_ref, mask2.at[:, cols(core * TOK, TOK)], ls.at[CH + 4])
-    for c in (w_copy, k_copy, v_copy, q_copy, m_copy):
+    for c in (w_copy, k_copy, v_copy, q_copy):
         c.start()
 
     pl.semaphore_wait(barrier, 9)
+
+    def out_copy(n, src, dst):
+        return pltpu.make_async_copy(src, dst, os_.at[n])
+
+    def layer_copy(i):
+        cc = cols(chunk(i) * WC, WC)
+        return out_copy(i, layer_ref.at[:, cc], layer_hbm.at[:, cc])
+
+    dq_copy = out_copy(CH, dq_ref, dq_hbm)
+    gw_copy = out_copy(CH + 1, gw_ref, gw_hbm)
+    dk_copy = out_copy(CH + 2, dk_ref, dk_hbm)
+    dv_copy = out_copy(CH + 3, dv_ref, dv_hbm)
 
     def stage_a(i):
         copy(AGY, i, cot_hbm.at[:, cols(chunk(i) * WC, WC)], cot.at[i, rows(t * 64, 64), :], par).start()
@@ -155,9 +168,17 @@
 
     other_heads = cols((1 - core) * 256, 256)
     q_send = extra(0, q_hbm.at[:, other_heads], q2.at[rows(core * TOK, TOK), :])
-    q_send.start()
-    m_send = extra(1, mask_ref, mask2.at[:, cols(core * TOK, TOK)])
-    m_send.start()
+    my_mask = mask2.at[:, cols(core * TOK, TOK)]
+    m_send = extra(1, my_mask, my_mask)
+
+    def prepare():
+        gh_acc[...] = jnp.zeros_like(gh_acc)
+        for tb in range(TOK // BLK):
+            for ab in range(AUD // BLK):
+                seen = jnp.full((1, BLK), mask_ref[tb, ab].astype(F32))
+                mask2[pl.ds(ab, 1), cols(core * TOK + tb * BLK, BLK)] = seen
+        q_send.start()
+        m_send.start()
 
     def kv_near(n, src_rows):
         heads = cols(((core + n) % 2) * 256, 256)
@@ -339,6 +360,7 @@
         got(YX, i, yr.at[i])
         total = reduced(i, yh) + yr[i].astype(F32)
         layer_ref[:, cols(chunk(i) * WC, WC)] = (gate * total).astype(BF)
+        layer_copy(i).start()
 
     def slot(i):
         return sum((i > n).astype(jnp.int32) for n in SCATTER_Y)
@@ -379,6 +401,27 @@
         got(R2, i, r2b.at[i, low, :])
         total = add_partner(i, x) + r1b[i, low, :].astype(F32) + r2b[i, low, :].astype(F32)
         layer_ref[:, cols(chunk(i) * WC, WC)] = (gate * total).astype(BF)
+        layer_copy(i).start()
+
+    def chunk_sent(i):
+        sent(AGY, i, cot.at[i, rows(x * 128, 64), :])
+
+        @pl.when(scatters_y(i))
+        def _():
+            for n in range(4):
+                sent(P0 + n, i, p4b.at[slot(i), n])
+            for kind in (F1, F2):
+                sent(kind, i, cot.at[i, rows(x * 128, 32), :])
+            for kind in (R1, R2):
+                sent(kind, i, cot.at[i, rows(x * 128, 64), :])
+
+        @pl.when(jnp.logical_not(scatters_y(i)))
+        def _():
+            sent(F1, i, f1b.at[i])
+            sent(F2, i, f2b.at[i])
+            sent(R1, i, r1b.at[i])
+            sent(R2, i, r2b.at[i])
+            sent(YX, i, ys.at[i])
 
     def scatters_y(i):
         return member(i, SCATTER_Y)
@@ -386,7 +429,11 @@
     stage_la = either(stage_la2, stage_la1, scatters_y)
     stage_lb = either(stage_lb2, stage_lb1, scatters_y)
     stage_lc = either(stage_lc2, stage_lc1, scatters_y)
-    stage_ld = either(stage_ld2, stage_ld1, scatters_y)
+    stage_ld_ = either(stage_ld2, stage_ld1, scatters_y)
+
+    def stage_ld(i):
+        stage_ld_(i)
+        chunk_sent(i)
 
     def masked(score, row, tok):
         return jnp.where(mask2[pl.ds(row, 1), tok] > 0, score, NEG)
@@ -440,6 +487,10 @@
             kv_red[hh, b] = total.astype(BF)
         for n in range(1, 4):
             kv_y(hh, n).start()
+        for dz in range(1, 4):
+            kv_z(hh, dz).wait_send()
+
+    kv_last = [idx for name, _, idx in PLAN if name == "KF"][0][-1]
 
     def kv_finish(hh):
         for n in range(1, 4):
@@ -452,6 +503,13 @@
         hc = cols((1 - core) * 256 + hh * HD, HD)
         dk_ref[:, hc] = other[:, :HD].astype(BF)
         dv_ref[:, hc] = other[:, HD:].astype(BF)
+        for n in range(1, 4):
+            kv_y(hh, n).wait_send()
+
+        @pl.when(hh == kv_last)
+        def _():
+            dk_copy.start()
+            dv_copy.start()
 
     gw_send = pltpu.make_async_remote_copy(
         src_ref=gw_sum, dst_ref=gw_par, send_sem=fs.at[0, 0], recv_sem=fr.at[0, 0],
@@ -488,6 +546,14 @@
             gw_ref[rr, :] = (gate * (total + gw_par[rr, :].astype(F32))).astype(BF)
 
         gw_reduce(0, write)
+        gw_copy.start()
+        gw_send.wait_send()
+
+        def gw_left(i, c):
+            sent(GW, i, gw_out.at[i])
+            return c
+
+        lax.fori_loop(2, CH, gw_left, 0)
 
     def backward(j):
         hh = j // 2
@@ -552,11 +618,8 @@
     gh_send = extra(3, gh_own.at[their_rows, :], gh2.at[:, cols(core * TOK, TOK)])
     dq_send = extra(4, dq_out, dq_in)
 
-    gh_acc[...] = jnp.zeros_like(gh_acc)
-
     def heads_first():
         q_copy.wait()
-        m_copy.wait()
         other_q = q2.at[rows((1 - core) * TOK, TOK), :]
         extra(0, other_q, other_q).wait_recv()
         other_m = mask2.at[:, cols((1 - core) * TOK, TOK)]
@@ -584,6 +647,13 @@
     def stage_hr():
         extra(2, ht.at[their_rows, :], ht.at[their_rows, :]).wait_recv()
         hrow[...] = ht[:, cols(core * TOK, TOK)].astype(F32).T.astype(BF)
+        q_send.wait_send()
+        m_send.wait_send()
+        ht_send.wait_send()
+        for n in range(1, 4):
+            for copy_ in kv_near(n, rows(s * 128, 128)):
+                copy_.wait_send()
+            kv_far(n, z).wait_send()
 
     def stage_gh():
         gh_own[...] = (gate * gh_acc[...]).astype(BF)
@@ -593,9 +663,12 @@
     def stage_df():
         dq_send.wait_recv()
         dq_ref[:, cols((1 - core) * 256, 256)] = dq_in[...]
+        dq_copy.start()
+        dq_send.wait_send()
+        gh_send.wait_send()
 
     once = {
-        "K0": kv_share, "K1": kv_spread, "HX": ht_send.start, "HR": stage_hr, "GH": stage_gh,
+        "L0": prepare, "K0": kv_share, "K1": kv_spread, "HX": ht_send.start, "HR": stage_hr, "GH": stage_gh,
         "GP": gw_part, "GF": gw_finish, "DQ": dq_send.start, "DF": stage_df,
     }
     each = {
@@ -635,56 +708,29 @@
     )
     lax.fori_loop(0, TICKS, tick, start)
 
-    def all_sent(i, c):
-        sent(AGY, i, cot.at[i, rows(x * 128, 64), :])
-
-        @pl.when(scatters_y(i))
-        def _():
-            for n in range(4):
-                sent(P0 + n, i, p4b.at[slot(i), n])
-            for kind in (F1, F2):
-                sent(kind, i, cot.at[i, rows(x * 128, 32), :])
-            for kind in (R1, R2):
-                sent(kind, i, cot.at[i, rows(x * 128, 64), :])
-
-        @pl.when(jnp.logical_not(scatters_y(i)))
-        def _():
-            sent(F1, i, f1b.at[i])
-            sent(F2, i, f2b.at[i])
-            sent(R1, i, r1b.at[i])
-            sent(R2, i, r2b.at[i])
-            sent(YX, i, ys.at[i])
-
-        @pl.when(i > 1)
-        def _():
-            sent(GW, i, gw_out.at[i])
-
+    def written(i, c):
+        layer_copy(i).wait()
         return c
 
-    lax.fori_loop(0, CH, all_sent, 0)
-    for n in range(1, 4):
-        for copy_ in kv_near(n, rows(s * 128, 128)):
-            copy_.wait_send()
-        kv_far(n, z).wait_send()
-        for hh in range(2):
-            kv_z(hh, n).wait_send()
-            kv_y(hh, n).wait_send()
-    gw_send.wait_send()
-    for c in (q_send, m_send, ht_send, gh_send, dq_send):
-        c.wait_send()
+    lax.fori_loop(0, CH, written, 0)
+    for c in (dq_copy, gw_copy, dk_copy, dv_copy):
+        c.wait()
 
 
 def hand_over(*refs):
-    sems = refs[10]
-    copies = [pltpu.make_async_copy(refs[n], refs[5 + n], sems.at[n]) for n in range(5)]
-    for c in copies:
+    given, results, held, sems = refs[:5], refs[5:10], refs[10:15], refs[15]
+    ins = [pltpu.make_async_copy(given[n], held[n], sems.at[0, n]) for n in range(5)]
+    outs = [pltpu.make_async_copy(held[n], results[n], sems.at[1, n]) for n in range(5)]
+    for c in ins:
         c.start()
-    for c in copies:
+    for c, d in zip(ins, outs):
         c.wait()
+        d.start()
+    for d in outs:
+        d.wait()
 
 
 def per_device(queries, audio_keys, audio_values, out_weight, mix_gate, block_mask, cotangent):
-    mask_rows = jnp.repeat(block_mask.T.astype(F32), BLK, axis=1)
     hbm = pl.BlockSpec(memory_space=pl.ANY)
     vmem = pl.BlockSpec(memory_space=pltpu.VMEM)
     dma = pltpu.SemaphoreType.DMA
@@ -697,9 +743,14 @@
             jax.ShapeDtypeStruct((128, 512), BF),
             jax.ShapeDtypeStruct((512, 512), BF),
         ),
-        in_specs=[hbm, hbm, hbm, hbm, vmem, vmem, hbm],
-        out_specs=[vmem] * 5,
+        in_specs=[hbm, hbm, hbm, hbm, vmem, pl.BlockSpec(memory_space=pltpu.SMEM), hbm],
+        out_specs=[hbm] * 5,
         scratch_shapes=[
+            pltpu.VMEM((64, 8192), BF),
+            pltpu.VMEM((TOK, 512), BF),
+            pltpu.VMEM((128, 512), BF),
+            pltpu.VMEM((128, 512), BF),
+            pltpu.VMEM((512, 512), BF),
             pltpu.VMEM((512, 8192), BF),
             pltpu.VMEM((CH, TOK, WC), BF),
             pltpu.VMEM((CH, TOK, HALF), BF),
@@ -739,19 +790,20 @@
             dma((2, 4)), dma((2, 4)),
             dma((2, 4)), dma((2, 4)),
             dma((5,)), dma((5,)),
-            dma((CH + 5,)),
+            dma((CH + 4,)),
+            dma((CH + 4,)),
         ],
         compiler_params=pltpu.CompilerParams(
             collective_id=0, has_side_effects=True, vmem_limit_bytes=62 * 2**20
         ),
         cost_estimate=pl.CostEstimate(flops=20 * 10**9, bytes_accessed=16 * 2**20, transcendentals=8 * 2**20),
-    )(queries, audio_keys, audio_values, out_weight, mix_gate.reshape(1, 1), mask_rows, cotangent)
+    )(queries, audio_keys, audio_values, out_weight, mix_gate.reshape(1, 1), block_mask, cotangent)
     return pl.pallas_call(
         hand_over,
         out_shape=tuple(jax.ShapeDtypeStruct(r.shape, r.dtype) for r in results),
-        in_specs=[vmem] * 5,
+        in_specs=[hbm] * 5,
         out_specs=[hbm] * 5,
-        scratch_shapes=[dma((5,))],
+        scratch_shapes=[pltpu.VMEM(r.shape, r.dtype) for r in results] + [dma((2, 5))],
     )(*results)
 
 

time: 143 us -> 138 us (0.965)
  Pallas kernels: 140 us -> 137 us
    pallas_call x1, Pallas kernels: 137 us -> 134 us  [per_device(): pl.pallas_call(kernel, out_shape=(jax.ShapeDtypeStruct((64, 8192), BF), j...]
where the time goes in v4:
time: 138 us
  Pallas kernels  137 us (99%)
    pallas_call x1, Pallas kernels, per_device(): pl.pallas_call(kernel, out_shape=(jax.ShapeDtypeStruct((64, 8192), BF), j...  134 us

profile of v4, /device:TPU:1, one launch (start us, length us, event | category | flops | bytes accessed | tf_op | source)
XLA Modules:
  0.0 137.8 jit_solution(3079632247412309752)
XLA Ops:
  1.3 133.8 %shard_map.110 = (bf16[64,8192]{1,0:T(8,128)(2,1)}, bf16[512,512]{1,0:T(8,128)(2,1)}, bf16[128,512]{1,0:T(8,128)(2,1)}, bf16[128,512]{1,0:T(8,128)(2,1)}, bf16[512,512]{1,0:T(8,128)(2,1)}) custom-call(bf16[512,512]{1,0:T(8,128)(2,1)} %q_hbm.1, bf16[128,512]{1,0:T(8,128)(2,1)} %k_hbm.1, bf16[128,512]{1,0:T(8,128)(2,1)} %v_hbm.1, bf16[512,8192]{1,0:T(8,128)(2,1)} %w_hbm.1, ...), custom_call_target="tpu_custom_call" | custom-call | flops 20000000000 | bytes 16777216 | tf_op jit(solution)/shard_map/pallas_call | solution.py:737
  135.1 2.7 %shard_map.111 = (bf16[64,8192]{1,0:T(8,128)(2,1)}, bf16[512,512]{1,0:T(8,128)(2,1)}, bf16[128,512]{1,0:T(8,128)(2,1)}, bf16[128,512]{1,0:T(8,128)(2,1)}, bf16[512,512]{1,0:T(8,128)(2,1)}) custom-call(bf16[64,8192]{1,0:T(8,128)(2,1)} %get-tuple-element.10.refs_0_, bf16[512,512]{1,0:T(8,128)(2,1)} %get-tuple-element.11.refs_1_, ...), custom_call_target="tpu_custom_call" | custom-call | tf_op jit(solution)/shard_map/pallas_call | solution.py:801

commit v5 on v4

--- a/solution.py
+++ b/solution.py
@@ -63,11 +63,10 @@
 
 def kernel(
     q_hbm, k_hbm, v_hbm, w_hbm, gate_ref, mask_ref, cot_hbm,
-    layer_hbm, dq_hbm, dk_hbm, dv_hbm, gw_hbm,
     layer_ref, dq_ref, dk_ref, dv_ref, gw_ref,
     w, cot, cot_sib, kvb, q2, mask2, ht, hrow, gh_acc, gh_own, gh2,
-    sc, pb, lse, delta, dq_acc, dq_out, dq_in, f1b, f2b, r1b, r2b, ys, yr, p4b, gw_out, gw_in, gw_sum, gw_par, kv_out, kv_in, kv_red, kv_fin,
-    ss, rs, ps, pr, zs, zr, ds_, dr, fs, fr, es, er, ls, os_,
+    sc, pb, lse, delta, dq_acc, dq_out, dq_in, f1b, f2b, r1b, r2b, yr, p4b, gw_out, gw_in, gw_par, kv_out, kv_in, kv_fin,
+    ss, rs, ps, pr, zs, zr, ds_, dr, fs, fr, es, er, ls,
 ):
     s = lax.axis_index("seq")
     t = lax.axis_index("tp")
@@ -139,18 +138,6 @@
 
     pl.semaphore_wait(barrier, 9)
 
-    def out_copy(n, src, dst):
-        return pltpu.make_async_copy(src, dst, os_.at[n])
-
-    def layer_copy(i):
-        cc = cols(chunk(i) * WC, WC)
-        return out_copy(i, layer_ref.at[:, cc], layer_hbm.at[:, cc])
-
-    dq_copy = out_copy(CH, dq_ref, dq_hbm)
-    gw_copy = out_copy(CH + 1, gw_ref, gw_hbm)
-    dk_copy = out_copy(CH + 2, dk_ref, dk_hbm)
-    dv_copy = out_copy(CH + 3, dv_ref, dv_hbm)
-
     def stage_a(i):
         copy(AGY, i, cot_hbm.at[:, cols(chunk(i) * WC, WC)], cot.at[i, rows(t * 64, 64), :], par).start()
 
@@ -353,14 +340,14 @@
     def stage_lc1(i):
         got(R1, i, r1b.at[i])
         got(R2, i, r2b.at[i])
-        ys[i] = reduced(i, 1 - yh).astype(BF)
-        copy(YX, i, ys.at[i], yr.at[i], par).start()
+        rr = rows(x * 128 + (1 - yh) * 64, 64)
+        cot[i, rr, :] = reduced(i, 1 - yh).astype(BF)
+        copy(YX, i, cot.at[i, rr, :], yr.at[i], par).start()
 
     def stage_ld1(i):
         got(YX, i, yr.at[i])
         total = reduced(i, yh) + yr[i].astype(F32)
         layer_ref[:, cols(chunk(i) * WC, WC)] = (gate * total).astype(BF)
-        layer_copy(i).start()
 
     def slot(i):
         return sum((i > n).astype(jnp.int32) for n in SCATTER_Y)
@@ -401,7 +388,6 @@
         got(R2, i, r2b.at[i, low, :])
         total = add_partner(i, x) + r1b[i, low, :].astype(F32) + r2b[i, low, :].astype(F32)
         layer_ref[:, cols(chunk(i) * WC, WC)] = (gate * total).astype(BF)
-        layer_copy(i).start()
 
     def chunk_sent(i):
         sent(AGY, i, cot.at[i, rows(x * 128, 64), :])
@@ -421,7 +407,7 @@
             sent(F2, i, f2b.at[i])
             sent(R1, i, r1b.at[i])
             sent(R2, i, r2b.at[i])
-            sent(YX, i, ys.at[i])
+            sent(YX, i, yr.at[i])
 
     def scatters_y(i):
         return member(i, SCATTER_Y)
@@ -474,7 +460,7 @@
     def kv_y(hh, n):
         src = ((yl + n // 2) % 2) * 2 + (core + n) % 2
         return pltpu.make_async_remote_copy(
-            src_ref=kv_red.at[hh, src], dst_ref=kv_fin.at[hh, n],
+            src_ref=kv_out.at[hh, rows(z * 512 + src * 128, 128), :], dst_ref=kv_fin.at[hh, n],
             send_sem=fs.at[hh, n], recv_sem=fr.at[hh, n], device_id=near(n), device_id_type=MESH)
 
     def kv_reduce(hh):
@@ -484,18 +470,16 @@
             total = kv_out[hh, rows(z * 512 + b * 128, 128), :].astype(F32)
             for dz in range(3):
                 total += kv_in[hh, dz, b * 128 : (b + 1) * 128, :].astype(F32)
-            kv_red[hh, b] = total.astype(BF)
+            kv_out[hh, rows(z * 512 + b * 128, 128), :] = total.astype(BF)
         for n in range(1, 4):
             kv_y(hh, n).start()
         for dz in range(1, 4):
             kv_z(hh, dz).wait_send()
 
-    kv_last = [idx for name, _, idx in PLAN if name == "KF"][0][-1]
-
     def kv_finish(hh):
         for n in range(1, 4):
             kv_y(hh, n).wait_recv()
-        same = kv_red[hh, yl * 2 + core].astype(F32) + kv_fin[hh, 2].astype(F32)
+        same = kv_out[hh, rows(s * 128, 128), :].astype(F32) + kv_fin[hh, 2].astype(F32)
         other = kv_fin[hh, 1].astype(F32) + kv_fin[hh, 3].astype(F32)
         hc = cols(core * 256 + hh * HD, HD)
         dk_ref[:, hc] = same[:, :HD].astype(BF)
@@ -506,13 +490,8 @@
         for n in range(1, 4):
             kv_y(hh, n).wait_send()
 
-        @pl.when(hh == kv_last)
-        def _():
-            dk_copy.start()
-            dv_copy.start()
-
     gw_send = pltpu.make_async_remote_copy(
-        src_ref=gw_sum, dst_ref=gw_par, send_sem=fs.at[0, 0], recv_sem=fr.at[0, 0],
+        src_ref=gw_out.at[1], dst_ref=gw_par, send_sem=fs.at[0, 0], recv_sem=fr.at[0, 0],
         device_id=near(2), device_id_type=MESH)
 
     def gw_reduce(which, write):
@@ -534,7 +513,7 @@
 
     def gw_part():
         def write(rr, total):
-            gw_sum[rr, :] = total.astype(BF)
+            gw_out[1, rr, :] = total.astype(BF)
 
         gw_reduce(1, write)
         gw_send.start()
@@ -546,7 +525,6 @@
             gw_ref[rr, :] = (gate * (total + gw_par[rr, :].astype(F32))).astype(BF)
 
         gw_reduce(0, write)
-        gw_copy.start()
         gw_send.wait_send()
 
         def gw_left(i, c):
@@ -663,7 +641,6 @@
     def stage_df():
         dq_send.wait_recv()
         dq_ref[:, cols((1 - core) * 256, 256)] = dq_in[...]
-        dq_copy.start()
         dq_send.wait_send()
         gh_send.wait_send()
 
@@ -708,26 +685,14 @@
     )
     lax.fori_loop(0, TICKS, tick, start)
 
-    def written(i, c):
-        layer_copy(i).wait()
-        return c
-
-    lax.fori_loop(0, CH, written, 0)
-    for c in (dq_copy, gw_copy, dk_copy, dv_copy):
+
+def hand_over(*refs):
+    given, results, sems = refs[:5], refs[5:10], refs[10]
+    outs = [pltpu.make_async_copy(given[n], results[n], sems.at[n]) for n in range(5)]
+    for c in outs:
+        c.start()
+    for c in outs:
         c.wait()
-
-
-def hand_over(*refs):
-    given, results, held, sems = refs[:5], refs[5:10], refs[10:15], refs[15]
-    ins = [pltpu.make_async_copy(given[n], held[n], sems.at[0, n]) for n in range(5)]
-    outs = [pltpu.make_async_copy(held[n], results[n], sems.at[1, n]) for n in range(5)]
-    for c in ins:
-        c.start()
-    for c, d in zip(ins, outs):
-        c.wait()
-        d.start()
-    for d in outs:
-        d.wait()
 
 
 def per_device(queries, audio_keys, audio_values, out_weight, mix_gate, block_mask, cotangent):
@@ -737,20 +702,15 @@
     results = pl.pallas_call(
         kernel,
         out_shape=(
-            jax.ShapeDtypeStruct((64, 8192), BF),
-            jax.ShapeDtypeStruct((TOK, 512), BF),
-            jax.ShapeDtypeStruct((128, 512), BF),
-            jax.ShapeDtypeStruct((128, 512), BF),
-            jax.ShapeDtypeStruct((512, 512), BF),
-        ),
-        in_specs=[hbm, hbm, hbm, hbm, vmem, pl.BlockSpec(memory_space=pltpu.SMEM), hbm],
-        out_specs=[hbm] * 5,
-        scratch_shapes=[
             pltpu.VMEM((64, 8192), BF),
             pltpu.VMEM((TOK, 512), BF),
             pltpu.VMEM((128, 512), BF),
             pltpu.VMEM((128, 512), BF),
             pltpu.VMEM((512, 512), BF),
+        ),
+        in_specs=[hbm, hbm, hbm, hbm, vmem, pl.BlockSpec(memory_space=pltpu.SMEM), hbm],
+        out_specs=[vmem] * 5,
+        scratch_shapes=[
             pltpu.VMEM((512, 8192), BF),
             pltpu.VMEM((CH, TOK, WC), BF),
             pltpu.VMEM((CH, TOK, HALF), BF),
@@ -774,15 +734,12 @@
             pltpu.VMEM((CH, 128, WC), BF),
             pltpu.VMEM((CH, 128, WC), BF),
             pltpu.VMEM((CH, 64, WC), BF),
-            pltpu.VMEM((CH, 64, WC), BF),
             pltpu.VMEM((3, 4, 64, WC), BF),
             pltpu.VMEM((CH, 512, HALF), BF),
             pltpu.VMEM((CH - 2, 512, HALF), BF),
             pltpu.VMEM((512, HALF), BF),
-            pltpu.VMEM((512, HALF), BF),
             pltpu.VMEM((2, AUD, 256), BF),
             pltpu.VMEM((2, 3, 512, 256), BF),
-            pltpu.VMEM((2, 4, 128, 256), BF),
             pltpu.VMEM((2, 4, 128, 256), BF),
             dma((KINDS, CH)), dma((KINDS, CH)),
             dma((4, 2)), dma((4, 2)),
@@ -791,19 +748,19 @@
             dma((2, 4)), dma((2, 4)),
             dma((5,)), dma((5,)),
             dma((CH + 4,)),
-            dma((CH + 4,)),
         ],
         compiler_params=pltpu.CompilerParams(
-            collective_id=0, has_side_effects=True, vmem_limit_bytes=62 * 2**20
+            collective_id=0, has_side_effects=True, vmem_limit_bytes=58 * 2**20
         ),
         cost_estimate=pl.CostEstimate(flops=20 * 10**9, bytes_accessed=16 * 2**20, transcendentals=8 * 2**20),
     )(queries, audio_keys, audio_values, out_weight, mix_gate.reshape(1, 1), block_mask, cotangent)
+    results = [pltpu.with_memory_space_constraint(r, pltpu.VMEM) for r in results]
     return pl.pallas_call(
         hand_over,
         out_shape=tuple(jax.ShapeDtypeStruct(r.shape, r.dtype) for r in results),
-        in_specs=[hbm] * 5,
+        in_specs=[vmem] * 5,
         out_specs=[hbm] * 5,
-        scratch_shapes=[pltpu.VMEM(r.shape, r.dtype) for r in results] + [dma((2, 5))],
+        scratch_shapes=[dma((5,))],
     )(*results)
 
 

time: 138 us -> 136 us (0.986)
  Pallas kernels: 137 us -> 134 us
where the time goes in v5:
time: 136 us
  Pallas kernels  134 us (99%)
    pallas_call x1, Pallas kernels, per_device(): pl.pallas_call(kernel, out_shape=(pltpu.VMEM((64, 8192), BF), pltpu.VMEM(...  133 us

profile of v5, /device:TPU:1, one launch (start us, length us, event | category | flops | bytes accessed | tf_op | source)
XLA Modules:
  0.0 135.7 jit_solution(4927410942962795472)
XLA Ops:
  1.3 133.0 %shard_map.110 = (bf16[64,8192]{1,0:T(8,128)(2,1)S(1)}, bf16[512,512]{1,0:T(8,128)(2,1)S(1)}, bf16[128,512]{1,0:T(8,128)(2,1)S(1)}, bf16[128,512]{1,0:T(8,128)(2,1)S(1)}, bf16[512,512]{1,0:T(8,128)(2,1)S(1)}) custom-call(bf16[512,512]{1,0:T(8,128)(2,1)} %q_hbm.1, bf16[128,512]{1,0:T(8,128)(2,1)} %k_hbm.1, bf16[128,512]{1,0:T(8,128)(2,1)} %v_hbm.1, ...), custom_call_target="tpu_custom_call" | custom-call | flops 20000000000 | bytes 16777216 | tf_op jit(solution)/shard_map/pallas_call | solution.py:702
  134.3 1.4 %shard_map.111 = (bf16[64,8192]{1,0:T(8,128)(2,1)}, bf16[512,512]{1,0:T(8,128)(2,1)}, bf16[128,512]{1,0:T(8,128)(2,1)}, bf16[128,512]{1,0:T(8,128)(2,1)}, bf16[512,512]{1,0:T(8,128)(2,1)}) custom-call(bf16[64,8192]{1,0:T(8,128)(2,1)S(1)} %get-tuple-element.10.refs_0_, bf16[512,512]{1,0:T(8,128)(2,1)S(1)} %get-tuple-element.11.refs_1_, ...), custom_call_target="tpu_custom_call" | custom-call | tf_op jit(solution)/shard_map/pallas_call | solution.py:758

commit v6 on v5

--- a/solution.py
+++ b/solution.py
@@ -27,33 +27,33 @@
 KINDS = P0 + 4
 GATHER_X = (3, 5)
 SCATTER_Y = (1, 3, 5)
-TICKS = 51
+TICKS = 54
 PLAN = (
-    ('HR', (18,), (0,)),
+    ('F', (18, 19, 22, 24, 28, 29, 30, 36), (5, 7, 3, 2, 0, 6, 1, 4)),
+    ('GP', (32,), (0,)),
+    ('B', (0, 1, 7, 8, 9, 10, 11, 15), (3, 5, 4, 2, 7, 0, 1, 6)),
+    ('D', (9, 10, 16, 17, 23, 24, 26, 28), (5, 3, 2, 7, 0, 4, 6, 1)),
+    ('GH', (29,), (0,)),
+    ('KF', (47, 48), (1, 0)),
+    ('X', (15, 17), (5, 3)),
+    ('E', (15, 19, 20, 22, 24, 25, 27, 28), (5, 7, 2, 3, 0, 4, 6, 1)),
     ('K0', (0,), (0,)),
-    ('A', (0, 2, 3, 4, 5, 6, 9, 10), (4, 2, 0, 7, 1, 3, 5, 6)),
-    ('GP', (32,), (0,)),
-    ('F', (18, 19, 22, 24, 27, 29, 30, 36), (5, 7, 3, 2, 0, 6, 1, 4)),
-    ('GH', (29,), (0,)),
-    ('B', (0, 1, 7, 8, 9, 10, 11, 15), (3, 5, 4, 2, 7, 0, 1, 6)),
-    ('X', (15, 17), (5, 3)),
-    ('LC', (32, 36, 40, 41, 42, 43, 44, 45), (5, 7, 0, 2, 1, 6, 3, 4)),
-    ('E', (15, 19, 20, 22, 24, 25, 26, 28), (5, 7, 2, 3, 0, 4, 6, 1)),
-    ('LB', (30, 31, 32, 33, 36, 37, 38, 39), (5, 2, 7, 0, 3, 6, 1, 4)),
-    ('D', (9, 10, 15, 16, 20, 23, 25, 27), (5, 3, 2, 7, 4, 0, 6, 1)),
-    ('LA', (18, 22, 23, 25, 28, 29, 31, 36), (5, 7, 3, 2, 0, 6, 1, 4)),
-    ('KF', (45, 47), (1, 0)),
-    ('KR', (38, 44), (0, 1)),
-    ('K1', (6,), (0,)),
-    ('DQ', (39,), (0,)),
-    ('LD', (43, 44, 45, 46, 47, 48, 49, 50), (5, 0, 1, 6, 7, 2, 4, 3)),
-    ('C', (4, 6, 9, 10, 11, 16, 20, 21), (3, 5, 2, 7, 4, 0, 6, 1)),
-    ('GF', (50,), (0,)),
+    ('LB', (30, 31, 32, 33, 37, 38, 39, 40), (5, 2, 7, 0, 3, 6, 1, 4)),
+    ('C', (4, 6, 9, 10, 11, 18, 20, 21), (3, 5, 2, 7, 4, 0, 6, 1)),
+    ('LA', (18, 22, 23, 26, 28, 29, 31, 36), (5, 7, 3, 2, 0, 6, 1, 4)),
+    ('A', (0, 1, 2, 3, 4, 5, 8, 9), (4, 2, 0, 7, 1, 3, 5, 6)),
+    ('BW', (31, 33, 34, 35), (0, 1, 2, 3)),
+    ('DQ', (40,), (0,)),
+    ('L0', (7,), (0,)),
     ('FW', (11, 12, 13, 14), (0, 1, 2, 3)),
+    ('LC', (36, 40, 41, 42, 43, 44, 45, 46), (7, 0, 5, 2, 1, 6, 3, 4)),
+    ('KR', (39, 45), (0, 1)),
+    ('LD', (45, 46, 48, 49, 50, 51, 52, 53), (0, 5, 1, 6, 7, 2, 4, 3)),
+    ('HR', (17,), (0,)),
+    ('GF', (53,), (0,)),
     ('HX', (14,), (0,)),
-    ('L0', (7,), (0,)),
-    ('DF', (42,), (0,)),
-    ('BW', (31, 33, 34, 35), (0, 1, 2, 3)),
+    ('K1', (5,), (0,)),
+    ('DF', (43,), (0,)),
 )
 
 
@@ -127,14 +127,11 @@
         own_piece(i).start()
         return c
 
-    lax.fori_loop(0, CH, start_piece, 0)
     w_copy = pltpu.make_async_copy(w_hbm, w, ls.at[CH])
     my_heads = cols(core * 256, 256)
     k_copy = pltpu.make_async_copy(k_hbm.at[:, my_heads], kvb.at[rows(s * 128, 128), pl.ds(0, 256)], ls.at[CH + 1])
     v_copy = pltpu.make_async_copy(v_hbm.at[:, my_heads], kvb.at[rows(s * 128, 128), pl.ds(256, 256)], ls.at[CH + 2])
     q_copy = pltpu.make_async_copy(q_hbm.at[:, my_heads], q2.at[rows(core * TOK, TOK), :], ls.at[CH + 3])
-    for c in (w_copy, k_copy, v_copy, q_copy):
-        c.start()
 
     pl.semaphore_wait(barrier, 9)
 
@@ -186,6 +183,12 @@
         for n in range(1, 4):
             for copy_ in kv_near(n, rows(s * 128, 128)):
                 copy_.start()
+
+        for c in (k_copy, v_copy):
+            c.start()
+        lax.fori_loop(0, CH, start_piece, 0)
+        for c in (q_copy, w_copy):
+            c.start()
 
     def kv_spread():
         k_copy.wait()

time: 136 us -> 134 us (0.985)
    pallas_call x1, Pallas kernels: 133 us -> 132 us  [per_device(): pl.pallas_call(kernel, out_shape=(pltpu.VMEM((64, 8192), BF), pltpu.VMEM(...]
where the time goes in v6:
time: 134 us
  Pallas kernels  133 us (99%)
    pallas_call x1, Pallas kernels, per_device(): pl.pallas_call(kernel, out_shape=(pltpu.VMEM((64, 8192), BF), pltpu.VMEM(...  132 us

profile of v6, /device:TPU:1, one launch (start us, length us, event | category | flops | bytes accessed | tf_op | source)
XLA Modules:
  0.0 134.3 jit_solution(9361361817988804750)
XLA Ops:
  1.3 131.6 %shard_map.110 = (bf16[64,8192]{1,0:T(8,128)(2,1)S(1)}, bf16[512,512]{1,0:T(8,128)(2,1)S(1)}, bf16[128,512]{1,0:T(8,128)(2,1)S(1)}, bf16[128,512]{1,0:T(8,128)(2,1)S(1)}, bf16[512,512]{1,0:T(8,128)(2,1)S(1)}) custom-call(bf16[512,512]{1,0:T(8,128)(2,1)} %q_hbm.1, bf16[128,512]{1,0:T(8,128)(2,1)} %k_hbm.1, bf16[128,512]{1,0:T(8,128)(2,1)} %v_hbm.1, ...), custom_call_target="tpu_custom_call" | custom-call | flops 20000000000 | bytes 16777216 | tf_op jit(solution)/shard_map/pallas_call | solution.py:705
  132.9 1.4 %shard_map.111 = (bf16[64,8192]{1,0:T(8,128)(2,1)}, bf16[512,512]{1,0:T(8,128)(2,1)}, bf16[128,512]{1,0:T(8,128)(2,1)}, bf16[128,512]{1,0:T(8,128)(2,1)}, bf16[512,512]{1,0:T(8,128)(2,1)}) custom-call(bf16[64,8192]{1,0:T(8,128)(2,1)S(1)} %get-tuple-element.10.refs_0_, bf16[512,512]{1,0:T(8,128)(2,1)S(1)} %get-tuple-element.11.refs_1_, ...), custom_call_target="tpu_custom_call" | custom-call | tf_op jit(solution)/shard_map/pallas_call | solution.py:761

commit v7 on v6

--- a/solution.py
+++ b/solution.py
@@ -24,7 +24,8 @@
 TN = (((0,), (0,)), ((), ()))
 
 AGY, AGP, AGM, AFP, AFM, SIB, GW, F1, F2, R1, R2, YX, YP, YM, YF, P0 = range(16)
-KINDS = P0 + 4
+R3, R4 = P0 + 4, P0 + 5
+KINDS = P0 + 6
 GATHER_X = (3, 5)
 SCATTER_Y = (1, 3, 5)
 TICKS = 54
@@ -323,14 +324,17 @@
         copy(F2, i, cot.at[i, rows(xf * 128 + 64, 64), :], f2b.at[i], prv).start()
 
     def stage_lb1(i):
+        top, low = pl.ds(0, 64), pl.ds(64, 64)
+        copy(R3, i, cot.at[i, rows(xn * 128 + 64, 64), :], r1b.at[i, low, :], nxt).start()
+        copy(R4, i, cot.at[i, rows(xb * 128, 64), :], r2b.at[i, top, :], prv).start()
         got(F1, i, f1b.at[i])
         rr = rows(xn * 128, 64)
         cot[i, rr, :] = (cot[i, rr, :].astype(F32) + f1b[i].astype(F32)).astype(BF)
-        copy(R1, i, cot.at[i, rows(xn * 128, 128), :], r1b.at[i], nxt).start()
+        copy(R1, i, cot.at[i, rr, :], r1b.at[i, top, :], nxt).start()
         got(F2, i, f2b.at[i])
         rr = rows(xb * 128 + 64, 64)
         cot[i, rr, :] = (cot[i, rr, :].astype(F32) + f2b[i].astype(F32)).astype(BF)
-        copy(R2, i, cot.at[i, rows(xb * 128, 128), :], r2b.at[i], prv).start()
+        copy(R2, i, cot.at[i, rr, :], r2b.at[i, low, :], prv).start()
 
     def reduced(i, which):
         rr = rows(which * 64, 64)
@@ -341,8 +345,11 @@
         )
 
     def stage_lc1(i):
-        got(R1, i, r1b.at[i])
-        got(R2, i, r2b.at[i])
+        top, low = pl.ds(0, 64), pl.ds(64, 64)
+        got(R1, i, r1b.at[i, top, :])
+        got(R3, i, r1b.at[i, low, :])
+        got(R2, i, r2b.at[i, low, :])
+        got(R4, i, r2b.at[i, top, :])
         rr = rows(x * 128 + (1 - yh) * 64, 64)
         cot[i, rr, :] = reduced(i, 1 - yh).astype(BF)
         copy(YX, i, cot.at[i, rr, :], yr.at[i], par).start()
@@ -408,8 +415,8 @@
         def _():
             sent(F1, i, f1b.at[i])
             sent(F2, i, f2b.at[i])
-            sent(R1, i, r1b.at[i])
-            sent(R2, i, r2b.at[i])
+            for kind in (R1, R2, R3, R4):
+                sent(kind, i, cot.at[i, rows(x * 128, 64), :])
             sent(YX, i, yr.at[i])
 
     def scatters_y(i):

time: 134 us -> 135 us (level)
  no operation moved by 1% of the time
where the time goes in v7:
time: 135 us
  Pallas kernels  133 us (99%)
    pallas_call x1, Pallas kernels, per_device(): pl.pallas_call(kernel, out_shape=(pltpu.VMEM((64, 8192), BF), pltpu.VMEM(...  132 us

profile of v7, /device:TPU:1, one launch (start us, length us, event | category | flops | bytes accessed | tf_op | source)
XLA Modules:
  0.0 134.6 jit_solution(16468675846096022795)
XLA Ops:
  1.3 131.8 %shard_map.110 = (bf16[64,8192]{1,0:T(8,128)(2,1)S(1)}, bf16[512,512]{1,0:T(8,128)(2,1)S(1)}, bf16[128,512]{1,0:T(8,128)(2,1)S(1)}, bf16[128,512]{1,0:T(8,128)(2,1)S(1)}, bf16[512,512]{1,0:T(8,128)(2,1)S(1)}) custom-call(bf16[512,512]{1,0:T(8,128)(2,1)} %q_hbm.1, bf16[128,512]{1,0:T(8,128)(2,1)} %k_hbm.1, bf16[128,512]{1,0:T(8,128)(2,1)} %v_hbm.1, ...), custom_call_target="tpu_custom_call" | custom-call | flops 20000000000 | bytes 16777216 | tf_op jit(solution)/shard_map/pallas_call | solution.py:712
  133.1 1.4 %shard_map.111 = (bf16[64,8192]{1,0:T(8,128)(2,1)}, bf16[512,512]{1,0:T(8,128)(2,1)}, bf16[128,512]{1,0:T(8,128)(2,1)}, bf16[128,512]{1,0:T(8,128)(2,1)}, bf16[512,512]{1,0:T(8,128)(2,1)}) custom-call(bf16[64,8192]{1,0:T(8,128)(2,1)S(1)} %get-tuple-element.10.refs_0_, bf16[512,512]{1,0:T(8,128)(2,1)S(1)} %get-tuple-element.11.refs_1_, ...), custom_call_target="tpu_custom_call" | custom-call | tf_op jit(solution)/shard_map/pallas_call | solution.py:768
